TPU v7x, 128 devices: a whole 4x4x4 slice. The times are simulated.
128 devices in a mesh: pp: 8 (over x, z_hi), ep: 16 (over y, z_lo, core).
Axes of the slice: x: 4, y: 4, z: 4 (z_hi: 2, z_lo: 2; z = z_hi * 2 + z_lo), core: 2. Of those that a mesh axis runs over, the one named last changes fastest.
Arguments:
- state_a: bfloat16 [8, 2048, 7168], P('pp', 'ep'), may hold values from -6 to 6
- state_b: bfloat16 [8, 2048, 7168], P('pp', 'ep'), may hold values from -6 to 6
- enter_a: bfloat16 [2048, 7168], P('ep'), may hold values from -6 to 6
- enter_b: bfloat16 [2048, 7168], P('ep'), may hold values from -6 to 6
- route_a: int32 [8, 2048, 1], P('pp', 'ep'), may hold values from 0 to 3; in each aligned block of 128 rows (0 to 127, 128 to 255, ..., all dimensions but the last counted through in order) at most 40 rows name the same one
- route_b: int32 [8, 2048, 1], P('pp', 'ep'), may hold values from 0 to 3; in each aligned block of 128 rows (0 to 127, 128 to 255, ..., all dimensions but the last counted through in order) at most 40 rows name the same one
- weight_a: float32 [8, 2048, 1], P('pp', 'ep'), may hold values from 0.5 to 2
- weight_b: float32 [8, 2048, 1], P('pp', 'ep'), may hold values from 0.5 to 2
- norm_gain: float32 [8, 7168], P('pp'), may hold values from 0.1 to 1.9
- w_gate: bfloat16 [8, 4096, 7168], P('pp', 'ep'), may hold values from -0.0625 to 0.0625
- w_up: bfloat16 [8, 4096, 7168], P('pp', 'ep'), may hold values from -0.0625 to 0.0625
- w_down: bfloat16 [8, 4096, 7168], P('pp', 'ep'), may hold values from -0.1875 to 0.1875
Outputs:
- new_a: bfloat16 [8, 2048, 7168], P('pp', 'ep')
- new_b: bfloat16 [8, 2048, 7168], P('pp', 'ep')
Inputs may be any that keep to these rules, and one draw needn't show every extreme that they name: `route_a`: among the routes of one device's 128 tokens at one section, no expert is named more than 40 times, a bound that some block reaches; every expert is named somewhere. `route_b`: as for route_a.
All inputs are finite; a program needn't handle non-finite values.
Results may differ from a plain program's by a relative error of at most 0.0054.
Values may be sent and summed in bfloat16 or wider, within the bound.
A program may use at most 256 MiB of HBM per device.

v0:
```python
import jax
import jax.numpy as jnp
from jax import lax
from jax.sharding import PartitionSpec as P

EGROUP = 4


def passed_along(block, axis, distance):
    devices = range(lax.axis_size(axis))
    route = [(i - distance, i) for i in devices if i - distance in devices]
    return lax.ppermute(block, axis, route)


def normalize(state, gain):
    widened = state.astype(jnp.float32)
    inverse = lax.rsqrt(jnp.mean(widened * widened, axis=-1, keepdims=True) + 1e-06)
    return (widened * inverse * gain).astype(jnp.bfloat16)


def slot_targets(flat_routes, experts, capacity):
    onehot = (flat_routes[:, None] == jnp.arange(experts, dtype=jnp.int32)[None, :]).astype(
        jnp.int32
    )
    earlier = jnp.cumsum(onehot, axis=0) - onehot
    return flat_routes * capacity + jnp.sum(earlier * onehot, axis=1)


def expert_apply(token_rows, w_gate, w_up, w_down):
    contract = (((1,), (1,)), ((), ()))
    gate_proj = lax.dot_general(token_rows, w_gate, contract, preferred_element_type=jnp.float32)
    up_proj = lax.dot_general(token_rows, w_up, contract, preferred_element_type=jnp.float32)
    hidden = (jax.nn.silu(gate_proj) * up_proj).astype(jnp.bfloat16)
    return jnp.dot(hidden, w_down, preferred_element_type=jnp.float32).astype(jnp.bfloat16)


def send_rows(buffer, w_gate, w_up, w_down):
    width = buffer.shape[2]
    outgoing = jnp.repeat(buffer, EGROUP, axis=0)
    received = lax.all_to_all(outgoing, "ep", split_axis=0, concat_axis=0, tiled=True)
    partial_value = expert_apply(received.reshape(-1, width), w_gate, w_up, w_down).reshape(
        received.shape
    )
    returned = lax.all_to_all(partial_value, "ep", split_axis=0, concat_axis=0, tiled=True)
    experts = buffer.shape[0]
    grouped = returned.reshape(experts, EGROUP, returned.shape[1], width)
    return jnp.sum(grouped.astype(jnp.float32), axis=1)


def local(
    state_a,
    state_b,
    enter_a,
    enter_b,
    route_a,
    route_b,
    weight_a,
    weight_b,
    norm_gain,
    w_gate,
    w_up,
    w_down,
):
    tok_rows = enter_a.shape[0]
    width = enter_a.shape[1]
    topk_count = route_a.shape[2]
    experts = lax.axis_size("ep") // EGROUP
    capacity = tok_rows * topk_count * 5 // (4 * experts)
    section_index = lax.axis_index("pp")
    section_count = lax.axis_size("pp")
    from_below = passed_along(state_a, "pp", 1)[0]
    from_above = passed_along(state_b, "pp", -1)[0]
    incoming_a = jnp.where(section_index == 0, enter_a, from_below)
    incoming_b = jnp.where(section_index == section_count - 1, enter_b, from_above)
    gain = norm_gain[0]
    gate_rows, up_rows, down_rows = (w_gate[0], w_up[0], w_down[0])

    def prepare(incoming, routes):
        normed = normalize(incoming, gain)
        target = slot_targets(routes.reshape(-1), experts, capacity)
        select = (
            jnp.arange(experts * capacity, dtype=jnp.int32)[:, None] == target[None, :]
        ).astype(jnp.bfloat16)
        repeated = jnp.repeat(normed, topk_count, axis=0)
        buffer = jnp.dot(select, repeated, preferred_element_type=jnp.float32).astype(jnp.bfloat16)
        return (target, buffer.reshape(experts, capacity, width))

    def finish(incoming, combined, target, weights):
        taken = jnp.take(combined.reshape(-1, width), target, axis=0).reshape(
            tok_rows, topk_count, width
        )
        branch = jnp.sum(taken * weights[:, :, None], axis=1)
        return (incoming.astype(jnp.float32) + branch).astype(jnp.bfloat16)

    target_a, buffer_a = prepare(incoming_a, route_a[0])
    target_b, buffer_b = prepare(incoming_b, route_b[0])
    combined_a = send_rows(buffer_a, gate_rows, up_rows, down_rows)
    combined_b = send_rows(buffer_b, gate_rows, up_rows, down_rows)
    result_a = finish(incoming_a, combined_a, target_a, weight_a[0])
    result_b = finish(incoming_b, combined_b, target_b, weight_b[0])
    return (result_a[None], result_b[None])


def solution(mesh):
    return jax.shard_map(
        local,
        mesh=mesh,
        in_specs=(
            P("pp", "ep", None),
            P("pp", "ep", None),
            P("ep", None),
            P("ep", None),
            P("pp", "ep", None),
            P("pp", "ep", None),
            P("pp", "ep", None),
            P("pp", "ep", None),
            P("pp", None),
            P("pp", "ep", None),
            P("pp", "ep", None),
            P("pp", "ep", None),
        ),
        out_specs=(P("pp", "ep", None), P("pp", "ep", None)),
        check_vma=False,
    )
```

profile of v0, /device:TPU:7, one launch (start us, length us, event | category | flops | bytes accessed | tf_op | source)
XLA Modules:
  0.0 690.7 jit_solution(4889943673575241873)
XLA Ops:
  0.6 0.0 copy-start.3
  0.6 5.8 collective-permute-start.1
  6.4 0.7 fusion.54
  7.2 0.2 reduce_window_sum.18
  7.3 0.8 select_reduce_fusion
  8.2 0.7 compare_and_fusion
  8.8 36.5 %collective-permute-done.1 = bf16[1,128,7168]{2,1,0:T(8,128)(2,1)} collective-permute-done((bf16[1,128,7168]{2,1,0:T(8,128)(2,1)}, bf16[1,128,7168]{2,1,0:T(8,128)(2,1)}, u32[]{:S(2)}, u32[]{:S(2)}) %collective-permute-start.1) | collective-permute-done | bytes 1835040 | tf_op jit(solution)/shard_map/ppermute | solution.py:12
  45.4 2.2 fusion.4
  47.6 0.0 copy-done.3
  47.7 0.8 convolution_convert_fusion.2
  48.5 4.7 broadcast_in_dim.31
  53.2 0.0 copy-start.4
  53.2 7.4 %all-to-all-start.2 = ((bf16[16,40,7168]{2,1,0:T(8,128)(2,1)}), bf16[16,40,7168]{2,1,0:T(8,128)(2,1)}, u32[]{:S(2)}, u32[]{:S(2)}) async-start(bf16[16,40,7168]{2,1,0:T(8,128)(2,1)} %bitcast.70), calls=%async_computation.2 | async-start | bytes 18350080 | tf_op jit(solution)/shard_map/all_to_all | solution.py:40
  60.5 2.3 collective-permute-start
  62.9 0.0 copy-done.4
  62.9 0.1 fusion.55
  63.0 0.2 reduce_window_sum.17
  63.1 0.2 select_reduce_fusion.1
  63.3 135.4 %collective-permute-done = bf16[1,128,7168]{2,1,0:T(8,128)(2,1)} collective-permute-done((bf16[1,128,7168]{2,1,0:T(8,128)(2,1)}, bf16[1,128,7168]{2,1,0:T(8,128)(2,1)}, u32[]{:S(2)}, u32[]{:S(2)}) %collective-permute-start) | collective-permute-done | bytes 1835040 | tf_op jit(solution)/shard_map/ppermute | solution.py:12
  198.8 2.2 fusion
  201.0 0.0 copy-start
  201.0 1.2 copy-done
  202.2 2.2 convolution_convert_fusion.3
  204.5 1.5 all-to-all-done.2
  206.0 6.4 broadcast_in_dim.17
  212.4 7.3 %all-to-all-start = ((bf16[16,40,7168]{2,1,0:T(8,128)(2,1)}), bf16[16,40,7168]{2,1,0:T(8,128)(2,1)}, u32[]{:S(2)}, u32[]{:S(2)}) async-start(bf16[16,40,7168]{2,1,0:T(8,128)(2,1)} %bitcast.71), calls=%async_computation | async-start | bytes 18350080 | tf_op jit(solution)/shard_map/all_to_all | solution.py:40
  219.7 7.2 %fusion.14 = f32[640,256]{1,0:T(8,128)S(1)} fusion(bf16[640,7168]{1,0:T(8,128)(2,1)} %bitcast.18, bf16[1,256,7168]{2,1,0:T(8,128)(2,1)} %param.23), kind=kOutput, calls=%fused_computation.28 | convolution fusion | flops 2348810240 | bytes 13500416 | tf_op jit(solution)/shard_map/dot_general | solution.py:31
  226.9 18.9 %convolution_convert_fusion = bf16[640,7168]{1,0:T(8,128)(2,1)} fusion(bf16[1,256,7168]{2,1,0:T(8,128)(2,1)} %param.25, bf16[640,7168]{1,0:T(8,128)(2,1)} %bitcast.18, bf16[1,256,7168]{2,1,0:T(8,128)(2,1)} %param.24, f32[640,256]{1,0:T(8,128)S(1)} %fusion.14), kind=kOutput, calls=%fused_computation.4 | convolution fusion | flops 4703191040 | bytes 26345472 | tf_op jit(solution)/shard_map/dot_general | solution.py:34
  245.8 119.0 %all-to-all-done = bf16[16,40,7168]{2,1,0:T(8,128)(2,1)} async-done(((bf16[16,40,7168]{2,1,0:T(8,128)(2,1)}), bf16[16,40,7168]{2,1,0:T(8,128)(2,1)}, u32[]{:S(2)}, u32[]{:S(2)}) %all-to-all-start) | async-done | bytes 9175072 | tf_op jit(solution)/shard_map/all_to_all | solution.py:40
  364.8 7.0 %all-to-all-start.3 = ((bf16[16,40,7168]{2,1,0:T(8,128)(2,1)}), bf16[16,40,7168]{2,1,0:T(8,128)(2,1)}, u32[]{:S(2)}, u32[]{:S(2)}) async-start(bf16[16,40,7168]{2,1,0:T(8,128)(2,1)} %bitcast.69), calls=%async_computation.3 | async-start | bytes 18350080 | tf_op jit(solution)/shard_map/all_to_all | solution.py:44
  371.8 7.2 %fusion.16 = f32[640,256]{1,0:T(8,128)S(1)} fusion(bf16[640,7168]{1,0:T(8,128)(2,1)} %bitcast.5, bf16[1,256,7168]{2,1,0:T(8,128)(2,1)} %param.23), kind=kOutput, calls=%fused_computation.30 | convolution fusion | flops 2348810240 | bytes 13500416 | tf_op jit(solution)/shard_map/dot_general | solution.py:31
  379.0 18.9 %convolution_convert_fusion.1 = bf16[640,7168]{1,0:T(8,128)(2,1)} fusion(bf16[1,256,7168]{2,1,0:T(8,128)(2,1)} %param.25, bf16[640,7168]{1,0:T(8,128)(2,1)} %bitcast.5, bf16[1,256,7168]{2,1,0:T(8,128)(2,1)} %param.24, f32[640,256]{1,0:T(8,128)S(1)} %fusion.16), kind=kOutput, calls=%fused_computation.5 | convolution fusion | flops 4703191040 | bytes 26345472 | tf_op jit(solution)/shard_map/dot_general | solution.py:34
  398.0 119.0 %all-to-all-done.3 = bf16[16,40,7168]{2,1,0:T(8,128)(2,1)} async-done(((bf16[16,40,7168]{2,1,0:T(8,128)(2,1)}), bf16[16,40,7168]{2,1,0:T(8,128)(2,1)}, u32[]{:S(2)}, u32[]{:S(2)}) %all-to-all-start.3) | async-done | bytes 9175072 | tf_op jit(solution)/shard_map/all_to_all | solution.py:44
  517.0 7.0 %all-to-all-start.1 = ((bf16[16,40,7168]{2,1,0:T(8,128)(2,1)}), bf16[16,40,7168]{2,1,0:T(8,128)(2,1)}, u32[]{:S(2)}, u32[]{:S(2)}) async-start(bf16[16,40,7168]{2,1,0:T(8,128)(2,1)} %bitcast.68), calls=%async_computation.1 | async-start | bytes 18350080 | tf_op jit(solution)/shard_map/all_to_all | solution.py:44
  524.1 8.1 %convert_reduce_fusion = f32[4,40,7168]{2,1,0:T(8,128)} fusion(bf16[16,40,7168]{2,1,0:T(8,128)(2,1)} %all-to-all-done.3), kind=kLoop, calls=%fused_computation.2 | loop fusion | flops 8028160 | bytes 13762560 | tf_op jit(solution)/shard_map/reduce_sum | solution.py:47
  532.2 7.3 %gather_fusion.1 = f32[128,7168]{1,0:T(8,128)} fusion(f32[160,7168]{1,0:T(8,128)} %bitcast.66, s32[1024]{0:T(1024)S(1)} %pad_clamp_fusion), kind=kCustom, calls=%fused_computation.1.clone | custom fusion | bytes 7340544 | tf_op jit(solution)/shard_map/jit(_take)/gather | solution.py:89
  539.5 129.6 %all-to-all-done.1 = bf16[16,40,7168]{2,1,0:T(8,128)(2,1)} async-done(((bf16[16,40,7168]{2,1,0:T(8,128)(2,1)}), bf16[16,40,7168]{2,1,0:T(8,128)(2,1)}, u32[]{:S(2)}, u32[]{:S(2)}) %all-to-all-start.1) | async-done | bytes 9175072 | tf_op jit(solution)/shard_map/all_to_all | solution.py:44
  669.2 8.0 %convert_reduce_fusion.1 = f32[4,40,7168]{2,1,0:T(8,128)} fusion(bf16[16,40,7168]{2,1,0:T(8,128)(2,1)} %all-to-all-done.1), kind=kLoop, calls=%fused_computation.3 | loop fusion | flops 8028160 | bytes 13762560 | tf_op jit(solution)/shard_map/reduce_sum | solution.py:47
  677.2 0.0 copy-start.5
  677.2 7.3 %gather_fusion = f32[128,7168]{1,0:T(8,128)} fusion(f32[160,7168]{1,0:T(8,128)} %bitcast.67, s32[1024]{0:T(1024)S(1)} %pad_clamp_fusion.1), kind=kCustom, calls=%fused_computation.clone | custom fusion | bytes 7340544 | tf_op jit(solution)/shard_map/jit(_take)/gather | solution.py:89
  684.5 0.0 copy-done.5
  684.5 0.0 copy-start.1
  684.5 0.0 copy-start.2
  684.5 0.0 copy-start.6
  684.5 4.1 fusion.18
  688.6 0.0 copy-done.1
  688.6 0.0 copy-done.2
  688.6 0.0 copy-done.6
  688.6 1.9 fusion.20
  (7 shorter events, 0.0 us)
Async XLA Ops:
  0.6 47.0 %copy-start.3 = (f32[1,7168]{1,0:T(1,128)S(1)}, f32[1,7168]{1,0:T(1,128)}, u32[]{:S(2)}) copy-start(f32[1,7168]{1,0:T(1,128)} %param.22) | copy-start | bytes 86020
  0.6 44.8 %collective-permute-start.1 = (bf16[1,128,7168]{2,1,0:T(8,128)(2,1)}, bf16[1,128,7168]{2,1,0:T(8,128)(2,1)}, u32[]{:S(2)}, u32[]{:S(2)}) collective-permute-start(bf16[1,128,7168]{2,1,0:T(8,128)(2,1)} %param.15), channel_id=1, source_target_pairs={{16,0},{32,16},{48,32},{64,48},{80,64},{96,80},{112,96},{17,1},{33... | collective-permute-start | bytes 5505032 | tf_op jit(solution)/shard_map/ppermute | solution.py:12
  53.2 9.7 %copy-start.4 = (s32[1,128,1]{1,2,0:T(1,128)S(1)}, s32[1,128,1]{1,2,0:T(1,128)}, u32[]{:S(2)}) copy-start(s32[1,128,1]{1,2,0:T(1,128)} %param.18) | copy-start | bytes 1540
  53.2 152.8 %all-to-all-start.2 = ((bf16[16,40,7168]{2,1,0:T(8,128)(2,1)}), bf16[16,40,7168]{2,1,0:T(8,128)(2,1)}, u32[]{:S(2)}, u32[]{:S(2)}) async-start(bf16[16,40,7168]{2,1,0:T(8,128)(2,1)} %bitcast.70), calls=%async_computation.2 | async-start | bytes 18350080 | tf_op jit(solution)/shard_map/all_to_all | solution.py:40
  60.5 138.2 %collective-permute-start = (bf16[1,128,7168]{2,1,0:T(8,128)(2,1)}, bf16[1,128,7168]{2,1,0:T(8,128)(2,1)}, u32[]{:S(2)}, u32[]{:S(2)}) collective-permute-start(bf16[1,128,7168]{2,1,0:T(8,128)(2,1)} %param.14), channel_id=1, source_target_pairs={{0,16},{16,32},{32,48},{48,64},{64,80},{80,96},{96,112},{1,17},{17... | collective-permute-start | bytes 5505032 | tf_op jit(solution)/shard_map/ppermute | solution.py:12
  201.0 1.2 copy-start
  212.4 152.4 %all-to-all-start = ((bf16[16,40,7168]{2,1,0:T(8,128)(2,1)}), bf16[16,40,7168]{2,1,0:T(8,128)(2,1)}, u32[]{:S(2)}, u32[]{:S(2)}) async-start(bf16[16,40,7168]{2,1,0:T(8,128)(2,1)} %bitcast.71), calls=%async_computation | async-start | bytes 18350080 | tf_op jit(solution)/shard_map/all_to_all | solution.py:40
  364.8 152.1 %all-to-all-start.3 = ((bf16[16,40,7168]{2,1,0:T(8,128)(2,1)}), bf16[16,40,7168]{2,1,0:T(8,128)(2,1)}, u32[]{:S(2)}, u32[]{:S(2)}) async-start(bf16[16,40,7168]{2,1,0:T(8,128)(2,1)} %bitcast.69), calls=%async_computation.3 | async-start | bytes 18350080 | tf_op jit(solution)/shard_map/all_to_all | solution.py:44
  517.0 152.2 %all-to-all-start.1 = ((bf16[16,40,7168]{2,1,0:T(8,128)(2,1)}), bf16[16,40,7168]{2,1,0:T(8,128)(2,1)}, u32[]{:S(2)}, u32[]{:S(2)}) async-start(bf16[16,40,7168]{2,1,0:T(8,128)(2,1)} %bitcast.68), calls=%async_computation.1 | async-start | bytes 18350080 | tf_op jit(solution)/shard_map/all_to_all | solution.py:44
  677.2 7.3 %copy-start.5 = (f32[1,128,1]{1,2,0:T(1,128)S(1)}, f32[1,128,1]{1,2,0:T(1,128)}, u32[]{:S(2)}) copy-start(f32[1,128,1]{1,2,0:T(1,128)} %param.21) | copy-start | bytes 1540
  684.5 4.1 copy-start.1
  684.5 4.1 copy-start.2
  684.5 4.1 copy-start.6
where the time goes:
time: 705 us; the launch traced here: 691 us
  waiting for transfers between devices  541 us (77%)
  matrix products  55.4 us (8%)
  starting transfers between devices  36.8 us (5%)
  other arithmetic  29.4 us (4%)
  local copies, waits for them, and re-layouts  26.9 us (4%)
    all_to_all x2, waiting for transfers between devices, send_rows(): lax.all_to_all(partial_value, 'ep', split_axis=0, concat_axis=0, tiled=True)  249 us
    ppermute x2, waiting for transfers between devices, passed_along(): return lax.ppermute(block, axis, route)  172 us
    all_to_all x2, waiting for transfers between devices, send_rows(): lax.all_to_all(outgoing, 'ep', split_axis=0, concat_axis=0, tiled=True)  121 us
    dot_general x2, matrix products, expert_apply(): jnp.dot(hidden, w_down, preferred_element_type=jnp.float32)  37.9 us
    reduce_sum x2, other arithmetic, send_rows(): return jnp.sum(grouped.astype(jnp.float32), axis=1)  16.1 us
    all_to_all x2, starting transfers between devices, send_rows(): lax.all_to_all(outgoing, 'ep', split_axis=0, concat_axis=0, tiled=True)  14.6 us
    gather x2, local copies, waits for them, and re-layouts, finish(): jnp.take(combined.reshape(-1, width), target, axis=0)  14.6 us
    dot_general x2, matrix products, expert_apply(): lax.dot_general(token_rows, w_gate, contract, preferred_element_type=jnp....  14.4 us
  transfers between devices with their start and end apart: 6, of which 6 were waited for; matrix products, arithmetic and copies ran while one was open for 11% of the time, Pallas kernels for 0%

commit v1 on v0

v1 whole, which is shorter than its diff:
```python
import functools

import jax
import jax.numpy as jnp
from jax import lax
from jax.experimental import pallas as pl
from jax.experimental.pallas import tpu as pltpu
from jax.sharding import PartitionSpec as P

EGROUP = 4
MESH = pl.DeviceIdType.MESH
BF16 = jnp.bfloat16
F32 = jnp.float32

HOPS = 8
SEND_COLS = 1024
OUT_COLS = 512


def iota(shape, dim):
    return lax.broadcasted_iota(jnp.int32, shape, dim)


def copy_wait(ref, sem):
    pltpu.make_async_copy(ref, ref, sem).wait()


def relay_kernel(
    sections,
    route_ref,
    gain_ref,
    state_a,
    state_b,
    enter_a,
    enter_b,
    w_gate,
    w_up,
    w_down,
    home_a,
    home_b,
    returned,
    xbuf,
    tgt_own,
    tgt_far,
    inv_ref,
    sel_ref,
    sendbuf,
    rows_ref,
    wgu,
    wd,
    acc,
    hs,
    hid,
    local_sem,
    tgt_sems,
    hi_send,
    arr_sem,
    home_sem,
    lo_send,
    out_sem,
    disp_send,
    disp_recv,
    disp_local,
    core_send,
    core_recv,
    hid_send,
    hid_recv,
    wd_send,
    wd_recv,
    ret_send,
    ret_recv,
):
    tok, width = state_a.shape
    share = w_gate.shape[0]
    half = width // 2
    cap2 = sendbuf.shape[2]
    cap = cap2 // 2
    chunk = tok // HOPS
    send_steps = width // SEND_COLS
    out_steps = half // OUT_COLS
    states, enters, homes = (state_a, state_b), (enter_a, enter_b), (home_a, home_b)

    p = lax.axis_index("pp")
    ep = lax.axis_index("ep")
    y, z, c = ep // 4, (ep // 2) % 2, ep % 2
    last = sections - 1

    def at(yy, zz, cc):
        return (p, yy * 4 + zz * 2 + cc)

    def turn(d):
        return (y + d) % 4

    far = y * 4 + (1 - z) * 2 + c
    first = (p == 0, p == last)
    ahead = (p + 1, p - 1)
    goes = (p < last, p > 0)

    load_gate = pltpu.make_async_copy(w_gate, wgu.at[pl.ds(0, share)], local_sem.at[0])
    load_up = pltpu.make_async_copy(w_up, wgu.at[pl.ds(share, share)], local_sem.at[1])
    part = z * 2 + c
    own_cols = pl.ds(pl.multiple_of(c * half, 128), half)
    load_down = pltpu.make_async_copy(w_down.at[:, own_cols], wd.at[part], local_sem.at[2])
    load_gate.start()
    load_up.start()
    load_down.start()

    barrier = pltpu.get_barrier_semaphore()

    def greet(device):
        pl.semaphore_signal(barrier, inc=1, device_id=device, device_id_type=MESH)

    for d in range(4):
        for cc in range(2):
            if d or cc:
                greet(at(turn(d), z, (c + cc) % 2))
    greet(at(y, 1 - z, c))
    greet(at(y, 1 - z, 1 - c))
    for s in range(2):

        @pl.when(goes[s])
        def _():
            greet((ahead[s], far))

    pl.semaphore_wait(barrier, 9 + (p + last - 1) // last + (2 * last - 1 - p) // last)

    def rows_of(i):
        return pl.ds(pl.multiple_of(i * chunk, chunk), chunk)

    def hop(s, i):
        return pltpu.make_async_remote_copy(
            states[s].at[rows_of(i)],
            xbuf.at[s, 1, rows_of(i)],
            hi_send.at[s],
            arr_sem.at[s, i],
            device_id=(ahead[s], far),
            device_id_type=MESH,
        )

    def enter_across(s, i):
        return pltpu.make_async_remote_copy(
            enters[s].at[rows_of(i)],
            xbuf.at[s, 1, rows_of(i)],
            lo_send.at[s],
            arr_sem.at[s, i],
            device_id=(p, far),
            device_id_type=MESH,
        )

    def enter_here(s, i):
        return pltpu.make_async_copy(
            enters[s].at[rows_of(i)], xbuf.at[s, 0, rows_of(i)], home_sem.at[s, i]
        )

    def across(s, i):
        return pltpu.make_async_remote_copy(
            xbuf.at[s, 1, rows_of(i)],
            xbuf.at[s, 0, rows_of(i)],
            lo_send.at[s],
            home_sem.at[s, i],
            device_id=(p, far),
            device_id_type=MESH,
        )

    def begin(s):
        @pl.when(goes[s])
        def _():
            @pl.loop(0, HOPS)
            def _(i):
                hop(s, i).start()

        @pl.when(first[s])
        def _():
            @pl.loop(0, HOPS)
            def _(i):
                enter_across(s, i).start()
                enter_here(s, i).start()

    def wd_copy(k, n):
        zz, cc = (z, 1 - c) if k == 0 else (1 - z, c if k == 1 else 1 - c)
        cols = pl.ds(pl.multiple_of(cc * half + n * OUT_COLS, 128), OUT_COLS)
        return pltpu.make_async_remote_copy(
            w_down.at[:, cols],
            wd.at[part, :, pl.ds(pl.multiple_of(n * OUT_COLS, 128), OUT_COLS)],
            wd_send.at[k],
            wd_recv.at[k, n],
            device_id=at(y, zz, cc),
            device_id_type=MESH,
        )

    def wd_wait(k, n):
        zz, cc = (z, 1 - c) if k == 0 else (1 - z, c if k == 1 else 1 - c)
        copy_wait(
            wd.at[zz * 2 + cc, :, pl.ds(pl.multiple_of(n * OUT_COLS, 128), OUT_COLS)],
            wd_recv.at[k, n],
        )

    begin(0)

    tri = (iota((tok, tok), 0) < iota((tok, tok), 1)).astype(BF16)
    slot_rows = []
    for s in range(2):
        route = route_ref[s : s + 1, :]
        onehot = (iota((16, tok), 0) == route).astype(F32)
        earlier = jnp.dot(onehot.astype(BF16), tri, preferred_element_type=F32)
        rank = jnp.sum(onehot * earlier, axis=0, keepdims=True)
        slot_rows.append(route.astype(F32) * cap + rank)
    tgt_own[...] = jnp.concatenate(slot_rows + [jnp.zeros((6, tok), F32)], axis=0)
    tgt_copy = pltpu.make_async_remote_copy(
        tgt_own,
        tgt_far,
        tgt_sems.at[0],
        tgt_sems.at[1],
        device_id=(p, far),
        device_id_type=MESH,
    )
    tgt_copy.start()

    def stats(s, rel, i):
        block = xbuf[s, rel, rows_of(i), :].astype(F32)
        mean = jnp.mean(block * block, axis=-1, keepdims=True)
        inv_ref[pl.ds(pl.multiple_of(rel * tok + i * chunk, chunk), chunk), :] = jnp.broadcast_to(
            lax.rsqrt(mean + 1e-06), (chunk, 128)
        )

    def arrive(s):
        @pl.loop(0, HOPS)
        def _(i):
            copy_wait(xbuf.at[s, 1, rows_of(i)], arr_sem.at[s, i])

            @pl.when(jnp.logical_not(first[s]))
            def _():
                across(s, i).start()

            if s == 0:

                @pl.when(i == HOPS - 2)
                def _():
                    begin(1)

            if s == 1:

                @pl.when(i == HOPS - 1)
                def _():
                    @pl.loop(0, out_steps)
                    def _(n):
                        for k in range(3):
                            wd_copy(k, n).start()

            stats(s, 1, i)

            @pl.when(i > 0)
            def _():
                copy_wait(xbuf.at[s, 0, rows_of(i - 1)], home_sem.at[s, i - 1])
                stats(s, 0, i - 1)

        copy_wait(xbuf.at[s, 0, rows_of(HOPS - 1)], home_sem.at[s, HOPS - 1])
        stats(s, 0, HOPS - 1)
        pltpu.make_async_copy(xbuf.at[s, 0], homes[s], out_sem.at[s]).start()

    def send_cols(j):
        return pl.ds(pl.multiple_of(j * SEND_COLS, 128), SEND_COLS)

    def disp(s, d, j):
        e = turn(d)
        return pltpu.make_async_remote_copy(
            sendbuf.at[s, e, :, send_cols(j)],
            rows_ref.at[s, c * 4 + y, :, send_cols(j)],
            disp_send.at[s, d - 1],
            disp_recv.at[s, d - 1, j],
            device_id=at(e, z, c),
            device_id_type=MESH,
        )

    def disp_here(s, j):
        return pltpu.make_async_copy(
            sendbuf.at[s, y, :, send_cols(j)],
            rows_ref.at[s, c * 4 + y, :, send_cols(j)],
            disp_local.at[s, j],
        )

    def dispatch(s):
        r = iota((4 * cap2, tok), 0)
        expert = sum((r >= cap2 * k).astype(jnp.int32) for k in range(1, 4))
        rem = r - expert * cap2
        rel = (rem >= cap).astype(jnp.int32)
        value = (expert * cap + rem - rel * cap).astype(F32)
        here = jnp.where((value == tgt_own[s : s + 1, :]) & (rel == 0), 1.0, 0.0)
        there = jnp.where((value == tgt_far[s : s + 1, :]) & (rel == 1), 1.0, 0.0)
        sel_ref[...] = jnp.concatenate([here, there], axis=1).astype(BF16)

        @pl.loop(0, send_steps)
        def _(j):
            for part_no in range(SEND_COLS // 512):
                cols = pl.ds(pl.multiple_of(j * SEND_COLS + part_no * 512, 128), 512)
                x = xbuf[s, :, :, cols].reshape(2 * tok, 512).astype(F32)
                normed = (x * inv_ref[:, 0:1] * gain_ref[:, cols]).astype(BF16)
                picked = jnp.dot(sel_ref[...], normed, preferred_element_type=F32)
                sendbuf[s, :, :, cols] = picked.astype(BF16).reshape(4, cap2, 512)
            for d in (1, 3, 2):
                disp(s, d, j).start()
            disp_here(s, j).start()

    def cores(s, j):
        block = rows_ref.at[s, pl.ds(c * 4, 4), :, send_cols(j)]
        return pltpu.make_async_remote_copy(
            block,
            block,
            core_send.at[s],
            core_recv.at[s, j],
            device_id=at(y, z, 1 - c),
            device_id_type=MESH,
        )

    def project(s, j):
        copy_wait(
            rows_ref.at[s, pl.ds((1 - c) * 4, 4), :, send_cols(j)], core_recv.at[s, j]
        )
        lhs = rows_ref[s, :, :, send_cols(j)].reshape(8 * cap2, SEND_COLS)
        acc[...] += lax.dot_general(
            lhs, wgu[:, send_cols(j)], (((1,), (1,)), ((), ())), preferred_element_type=F32
        )

    def hid_copy(s, k):
        zz, cc = (z, 1 - c) if k == 0 else (1 - z, c if k == 1 else 1 - c)
        return pltpu.make_async_remote_copy(
            hs.at[s, 0 if k == 0 else 1],
            hid.at[s, part],
            hid_send.at[s, k],
            hid_recv.at[s, k],
            device_id=at(y, zz, cc),
            device_id_type=MESH,
        )

    def hid_wait(s, k):
        zz, cc = (z, 1 - c) if k == 0 else (1 - z, c if k == 1 else 1 - c)
        copy_wait(hid.at[s, zz * 2 + cc], hid_recv.at[s, k])

    def hidden(s):
        acc[...] = jnp.zeros_like(acc)

        @pl.loop(0, send_steps)
        def _(j):
            for d in (1, 3, 2):
                copy_wait(
                    rows_ref.at[s, c * 4 + turn(4 - d), :, send_cols(j)],
                    disp_recv.at[s, d - 1, j],
                )
            disp_here(s, j).wait()
            cores(s, j).start()

            @pl.when(j > 0)
            def _():
                project(s, j - 1)

        project(s, send_steps - 1)
        gate, up = acc[:, :share], acc[:, share:]
        h = gate / (1.0 + jnp.exp(-gate)) * up
        mine = [h[b * cap2 : b * cap2 + cap] for b in range(8)]
        others = [h[b * cap2 + cap : (b + 1) * cap2] for b in range(8)]
        hs[s, 0] = jnp.concatenate(mine, axis=0).astype(BF16)
        hs[s, 1] = jnp.concatenate(others, axis=0).astype(BF16)
        for k in (1, 2, 0):
            hid_copy(s, k).start()
        hid[s, part] = hs[s, 0]

    def back(k, n):
        d, cc = k // 2, k % 2
        yy = turn(d)
        to = (c + cc) % 2
        src = sendbuf.at[0, yy, :, pl.ds(pl.multiple_of(to * half + n * OUT_COLS, 128), OUT_COLS)]
        dst = returned.at[y, :, pl.ds(pl.multiple_of(c * half + n * OUT_COLS, 128), OUT_COLS)]
        if k == 0:
            return pltpu.make_async_copy(src, dst, ret_recv.at[0])
        return pltpu.make_async_remote_copy(
            src, dst, ret_send.at[k], ret_recv.at[k], device_id=at(yy, z, to), device_id_type=MESH
        )

    def down(n):
        for k in range(3):
            wd_wait(k, n)
        cols = pl.ds(pl.multiple_of(n * OUT_COLS, 128), OUT_COLS)
        outs = []
        for s in range(2):
            out = jnp.zeros((8 * cap, OUT_COLS), F32)
            for g in range(EGROUP):
                out += jnp.dot(hid[s, g], wd[g, :, cols], preferred_element_type=F32)
            outs.append(out)
        for cc in range(2):
            rows = []
            for b in range(4 * cc, 4 * cc + 4):
                rows += [out[b * cap : (b + 1) * cap] for out in outs]
            to = pl.ds(pl.multiple_of(cc * half + n * OUT_COLS, 128), OUT_COLS)
            sendbuf[0, :, :, to] = (
                jnp.concatenate(rows, axis=0).astype(BF16).reshape(4, cap2, OUT_COLS)
            )
        for k in (2, 3, 6, 7, 4, 5, 1, 0):
            back(k, n).start()

    arrive(0)
    tgt_copy.wait()
    dispatch(0)
    arrive(1)
    dispatch(1)
    load_gate.wait()
    load_up.wait()
    hidden(0)
    hidden(1)
    load_down.wait()
    for s in range(2):
        for k in range(3):
            hid_wait(s, k)
    for d in (1, 2, 3):
        copy_wait(sendbuf.at[0, turn(d)], disp_send.at[0, d - 1])
    pl.loop(0, out_steps)(down)

    for s in range(2):

        @pl.when(goes[s])
        def _():
            copy_wait(states[s], hi_send.at[s])

        copy_wait(xbuf.at[s, 1], lo_send.at[s])
        pltpu.make_async_copy(xbuf.at[s, 0], homes[s], out_sem.at[s]).wait()
        copy_wait(rows_ref.at[s, pl.ds(c * 4, 4)], core_send.at[s])
        for k in range(3):
            copy_wait(hs.at[s, 0], hid_send.at[s, k])
    for d in (1, 2, 3):
        copy_wait(sendbuf.at[1, turn(d)], disp_send.at[1, d - 1])
    for k in range(3):
        copy_wait(wd.at[part], wd_send.at[k])
    for k in range(8):
        d, cc = k // 2, k % 2
        source = pl.ds(pl.multiple_of(((c + cc) % 2) * half, 128), half)
        copy_wait(returned.at[turn(4 - d), :, source], ret_recv.at[k])
        if k:
            copy_wait(sendbuf.at[0, turn(d), :, source], ret_send.at[k])


def finish_kernel(
    route_a, route_b, weight_a, weight_b, home_a, home_b, returned, new_a, new_b, sel_ref
):
    tok = route_a.shape[0]
    cap2 = returned.shape[1]
    cap = cap2 // 2
    slots = 4 * cap2

    @pl.when(pl.program_id(0) == 0)
    def _():
        tri = (iota((tok, tok), 1) < iota((tok, tok), 0)).astype(BF16)
        r = iota((tok, slots), 1)
        expert = sum((r >= cap2 * k).astype(jnp.int32) for k in range(1, 4))
        rem = r - expert * cap2
        stream = (rem >= cap).astype(jnp.int32)
        value = (expert * cap + rem - stream * cap).astype(F32)
        for s, route_ref in enumerate((route_a, route_b)):
            route = route_ref[...]
            onehot = (iota((tok, 128), 1) == route).astype(F32)
            earlier = jnp.dot(tri, onehot.astype(BF16), preferred_element_type=F32)
            rank = jnp.sum(onehot * earlier, axis=1, keepdims=True)
            target = route.astype(F32) * cap + rank
            sel_ref[s] = jnp.where((value == target) & (stream == s), 1.0, 0.0).astype(BF16)

    block = returned[...].reshape(slots, returned.shape[2])
    for s, (weight, home, new) in enumerate(
        ((weight_a, home_a, new_a), (weight_b, home_b, new_b))
    ):
        taken = jnp.dot(sel_ref[s], block, preferred_element_type=F32)
        new[...] = (home[...].astype(F32) + taken * weight[...]).astype(BF16)


def local(
    state_a,
    state_b,
    enter_a,
    enter_b,
    route_a,
    route_b,
    weight_a,
    weight_b,
    norm_gain,
    w_gate,
    w_up,
    w_down,
):
    tok, width = enter_a.shape
    sections = lax.axis_size("pp")
    experts = lax.axis_size("ep") // EGROUP
    cap = tok * 5 // (4 * experts)
    cap2 = 2 * cap
    half = width // 2
    share = w_gate.shape[1]
    send_steps = width // SEND_COLS
    out_steps = half // OUT_COLS
    routes = jnp.concatenate([route_a.reshape(1, tok), route_b.reshape(1, tok)], axis=0)
    hbm = pl.BlockSpec(memory_space=pl.ANY)
    vmem = pl.BlockSpec(memory_space=pltpu.VMEM)
    dma = pltpu.SemaphoreType.DMA
    home_a, home_b, returned = pl.pallas_call(
        functools.partial(relay_kernel, sections),
        out_shape=(
            jax.ShapeDtypeStruct((tok, width), BF16),
            jax.ShapeDtypeStruct((tok, width), BF16),
            jax.ShapeDtypeStruct((experts, cap2, width), BF16),
        ),
        in_specs=[vmem, vmem] + [hbm] * 7,
        out_specs=(hbm, hbm, hbm),
        scratch_shapes=[
            pltpu.VMEM((2, 2, tok, width), BF16),
            pltpu.VMEM((8, tok), F32),
            pltpu.VMEM((8, tok), F32),
            pltpu.VMEM((2 * tok, 128), F32),
            pltpu.VMEM((experts * cap2, 2 * tok), BF16),
            pltpu.VMEM((2, experts, cap2, width), BF16),
            pltpu.VMEM((2, 8, cap2, width), BF16),
            pltpu.VMEM((2 * share, width), BF16),
            pltpu.VMEM((EGROUP, share, half), BF16),
            pltpu.VMEM((8 * cap2, 2 * share), F32),
            pltpu.VMEM((2, 2, 8 * cap, share), BF16),
            pltpu.VMEM((2, EGROUP, 8 * cap, share), BF16),
            dma((3,)),
            dma((2,)),
            dma((2,)),
            dma((2, HOPS)),
            dma((2, HOPS)),
            dma((2,)),
            dma((2,)),
            dma((2, 3)),
            dma((2, 3, send_steps)),
            dma((2, send_steps)),
            dma((2,)),
            dma((2, send_steps)),
            dma((2, 3)),
            dma((2, 3)),
            dma((3,)),
            dma((3, out_steps)),
            dma((8,)),
            dma((8,)),
        ],
        compiler_params=pltpu.CompilerParams(
            collective_id=0, has_side_effects=True, vmem_limit_bytes=60 * 2**20
        ),
        name="relay",
    )(
        routes,
        norm_gain,
        state_a[0],
        state_b[0],
        enter_a,
        enter_b,
        w_gate[0],
        w_up[0],
        w_down[0],
    )
    cols = 1024
    whole = pl.BlockSpec((tok, 1), lambda j: (0, 0))
    piece = pl.BlockSpec((tok, cols), lambda j: (0, j))
    new_a, new_b = pl.pallas_call(
        finish_kernel,
        grid=(width // cols,),
        in_specs=[whole] * 4
        + [piece, piece, pl.BlockSpec((experts, cap2, cols), lambda j: (0, 0, j))],
        out_specs=(piece, piece),
        out_shape=(
            jax.ShapeDtypeStruct((tok, width), BF16),
            jax.ShapeDtypeStruct((tok, width), BF16),
        ),
        scratch_shapes=[pltpu.VMEM((2, tok, experts * cap2), BF16)],
        name="finish",
    )(route_a[0], route_b[0], weight_a[0], weight_b[0], home_a, home_b, returned)
    return (new_a[None], new_b[None])


def solution(mesh):
    return jax.shard_map(
        local,
        mesh=mesh,
        in_specs=(
            P("pp", "ep", None),
            P("pp", "ep", None),
            P("ep", None),
            P("ep", None),
            P("pp", "ep", None),
            P("pp", "ep", None),
            P("pp", "ep", None),
            P("pp", "ep", None),
            P("pp", None),
            P("pp", "ep", None),
            P("pp", "ep", None),
            P("pp", "ep", None),
        ),
        out_specs=(P("pp", "ep", None), P("pp", "ep", None)),
        check_vma=False,
    )
```

time: 705 us -> 297 us (0.42)
  the two profiles are of different devices: /device:TPU:7 before, /device:TPU:96 now
where the time goes in v1:
time: 297 us; the launch traced here: 296 us
  Pallas kernels  289 us (97%)
  local copies, waits for them, and re-layouts  5.55 us (2%)
    pallas_call x1, Pallas kernels, local(): pl.pallas_call(functools.partial(relay_kernel, sections), out_shape=(jax....  280 us
    pallas_call x1, Pallas kernels, local(): pl.pallas_call(finish_kernel, grid=(width // cols,), in_specs=[whole] * 4...  8.91 us

profile of v1, /device:TPU:96, one launch (start us, length us, event | category | flops | bytes accessed | tf_op | source)
XLA Modules:
  0.0 296.1 jit_solution(14560497499518976395)
XLA Ops:
  0.6 1.2 pad_add_fusion.route_ref
  1.9 1.4 copy.16.weight_a
  3.3 1.4 copy.17.weight_b
  4.6 1.4 copy.15.route_b
  6.0 1.4 copy.14.route_a
  7.4 279.8 %relay.1 = (bf16[128,7168]{1,0:T(8,128)(2,1)}, bf16[128,7168]{1,0:T(8,128)(2,1)}, bf16[4,80,7168]{2,1,0:T(8,128)(2,1)}) custom-call(s32[2,128]{1,0:T(2,128)} %pad_add_fusion.route_ref, f32[1,7168]{1,0:T(1,128)} %gain_ref.1, bf16[128,7168]{1,0:T(8,128)(2,1)} %bitcast.16, bf16[128,7168]{1,0:T(8,128)(2,1)} %bitcast.17, bf16[128,7168]{1,0:T(8,128)(2,1)} %enter_a.1, ...), custom_call_target="tpu_custom_call" | custom-call | tf_op jit(solution)/shard_map/relay/pallas_call | solution.py:499
  287.2 8.9 %finish.1 = (bf16[128,7168]{1,0:T(8,128)(2,1)}, bf16[128,7168]{1,0:T(8,128)(2,1)}) custom-call(s32[128,1]{1,0:T(8,128)} %copy.14.route_a, s32[128,1]{1,0:T(8,128)} %copy.15.route_b, f32[128,1]{1,0:T(8,128)} %copy.16.weight_a, f32[128,1]{1,0:T(8,128)} %copy.17.weight_b, bf16[128,7168]{1,0:T(8,128)(2,1)} %get-tuple-element.7.home_a, ...), custom_call_target="tpu_custom_call" | custom-call | tf_op jit(solution)/shard_map/finish/pallas_call | solution.py:558

commit v2 on v0

v2 whole, which is shorter than its diff:
```python
import functools

import jax
import jax.numpy as jnp
from jax import lax
from jax.experimental import pallas as pl
from jax.experimental.pallas import tpu as pltpu
from jax.sharding import PartitionSpec as P

EGROUP = 4
MESH = pl.DeviceIdType.MESH
BF16 = jnp.bfloat16
F32 = jnp.float32

STEP = 1024
OUT_COLS = 256
LAG = 7
EARLY = 6
BEHIND = 2


def iota(shape, dim):
    return lax.broadcasted_iota(jnp.int32, shape, dim)


def copy_wait(ref, sem):
    pltpu.make_async_copy(ref, ref, sem).wait()


def relay_kernel(
    sections,
    meta_ref,
    gain_ref,
    state_a,
    state_b,
    enter_a,
    enter_b,
    w_gate,
    w_up,
    w_down,
    new_a,
    new_b,
    stage,
    stat,
    wide_ref,
    inv_col,
    xbuf,
    inv_ref,
    tgt_own,
    tgt_far,
    sel_ref,
    pick_ref,
    weight_ref,
    sendbuf,
    returned,
    rows_ref,
    wgu,
    wd,
    acc,
    hs,
    hid,
    local_sem,
    tgt_sems,
    stage_sem,
    inv_sems,
    hi_send,
    arr_sem,
    home_sem,
    lo_send,
    out_sem,
    disp_send,
    disp_recv,
    disp_local,
    core_send,
    core_recv,
    hid_send,
    hid_recv,
    wd_send,
    wd_recv,
    ret_send,
    ret_recv,
):
    tok, width = state_a.shape
    share = w_gate.shape[0]
    half = width // 2
    cap2 = sendbuf.shape[1]
    cap = cap2 // 2
    steps = width // STEP
    total = 2 * steps
    out_steps = half // OUT_COLS

    p = lax.axis_index("pp")
    ep = lax.axis_index("ep")
    y, z, c = ep // 4, (ep // 2) % 2, ep % 2
    odd = p % 2
    inner = (p % (sections - 1) + sections - 2) // (sections - 1)
    edge = inner == 0
    hop_to = (p + inner * (2 * odd - 1), p + 1 - 2 * odd)
    far = y * 4 + (1 - z) * 2 + c
    part = z * 2 + c

    def at(yy, zz, cc):
        return (p, yy * 4 + zz * 2 + cc)

    def turn(d):
        return (y + d) % 4

    def remote(src, dst, send, recv, device):
        return pltpu.make_async_remote_copy(
            src, dst, send, recv, device_id=device, device_id_type=MESH
        )

    def cols_of(i, size, base=0):
        return pl.ds(pl.multiple_of(base + i * size, 128), size)

    def staging(t, ref):
        return pltpu.make_async_copy(ref, stage.at[t], stage_sem.at[t])

    @pl.when(edge & (odd == 0))
    def _():
        staging(0, enter_a).start()

    @pl.when(edge & (odd == 1))
    def _():
        staging(0, enter_b).start()

    @pl.when((inner == 1) & (odd == 0))
    def _():
        staging(0, state_b).start()

    @pl.when((inner == 1) & (odd == 1))
    def _():
        staging(0, state_a).start()

    @pl.when(odd == 0)
    def _():
        staging(1, state_a).start()

    @pl.when(odd == 1)
    def _():
        staging(1, state_b).start()

    barrier = pltpu.get_barrier_semaphore()

    def greet(device):
        pl.semaphore_signal(barrier, inc=1, device_id=device, device_id_type=MESH)

    for d in range(4):
        for cc in range(2):
            if d or cc:
                greet(at(turn(d), z, (c + cc) % 2))
    greet(at(y, 1 - z, c))
    greet(at(y, 1 - z, 1 - c))
    greet((hop_to[1], far))

    @pl.when(inner == 1)
    def _():
        greet((hop_to[0], far))

    pl.semaphore_wait(barrier, 10 + inner)

    def hop(t, j):
        cols = cols_of(j, STEP)
        return remote(
            stage.at[t, :, cols],
            xbuf.at[t, 1, :, cols],
            hi_send.at[t],
            arr_sem.at[t, j],
            (hop_to[t], far),
        )

    def enter_here(j):
        cols = cols_of(j, STEP)
        return pltpu.make_async_copy(
            stage.at[0, :, cols], xbuf.at[0, 0, :, cols], home_sem.at[0, j]
        )

    def across(t, j):
        cols = cols_of(j, STEP)
        return remote(
            xbuf.at[t, 1, :, cols],
            xbuf.at[t, 0, :, cols],
            lo_send.at[t],
            home_sem.at[t, j],
            (p, far),
        )

    def inv_hop(t):
        return remote(
            stat.at[t], inv_ref.at[t, 1], inv_sems.at[t, 0], inv_sems.at[t, 1], (hop_to[t], far)
        )

    def inv_here():
        return pltpu.make_async_copy(stat.at[0], inv_ref.at[0, 0], inv_sems.at[0, 3])

    def inv_across(t):
        return remote(
            inv_ref.at[t, 1], inv_ref.at[t, 0], inv_sems.at[t, 2], inv_sems.at[t, 3], (p, far)
        )

    def depart(t):
        @pl.loop(0, tok // 16)
        def _(i):
            rows = pl.ds(pl.multiple_of(i * 16, 16), 16)
            block = stage[t, rows, :].astype(F32)
            mean = jnp.mean(block * block, axis=-1, keepdims=True)
            wide_ref[rows, :] = jnp.broadcast_to(lax.rsqrt(mean + 1e-06), (16, 128))

        same = iota((tok, tok), 1) == iota((tok, tok), 0)
        line = jnp.sum(jnp.where(same, wide_ref[...], 0.0), axis=0, keepdims=True)
        stat[t] = jnp.broadcast_to(line, (8, tok))
        inv_hop(t).start()

        @pl.loop(1, steps)
        def _(j):
            hop(t, j).start()

        if t == 0:

            @pl.when(edge)
            def _():
                inv_here().start()

                @pl.loop(0, steps)
                def _(j):
                    enter_here(j).start()

    def wd_other(k):
        return (z, 1 - c) if k == 0 else (1 - z, c if k == 1 else 1 - c)

    def wd_copy(k, n):
        zz, cc = wd_other(k)
        return remote(
            w_down.at[:, cols_of(n, OUT_COLS, cc * half)],
            wd.at[part, :, cols_of(n, OUT_COLS)],
            wd_send.at[k],
            wd_recv.at[k, n],
            at(y, zz, cc),
        )

    def wd_wait(k, n):
        zz, cc = wd_other(k)
        copy_wait(wd.at[zz * 2 + cc, :, cols_of(n, OUT_COLS)], wd_recv.at[k, n])

    for k in (1, 2, 0):
        wd_copy(k, 0).start()
    copy_wait(stage.at[0], stage_sem.at[0])
    hop(0, 0).start()

    tri = (iota((tok, tok), 0) < iota((tok, tok), 1)).astype(BF16)
    slot_rows = []
    for t in range(2):
        route = jnp.where(odd == t, meta_ref[0:1, :], meta_ref[1:2, :])
        onehot = (iota((16, tok), 0).astype(F32) == route).astype(F32)
        earlier = jnp.dot(onehot.astype(BF16), tri, preferred_element_type=F32)
        rank = jnp.sum(onehot * earlier, axis=0, keepdims=True)
        slot_rows.append(route * cap + rank)
    tgt_own[...] = jnp.concatenate(slot_rows + [jnp.zeros((6, tok), F32)], axis=0)
    tgt_copy = remote(tgt_own, tgt_far, tgt_sems.at[0], tgt_sems.at[1], (p, far))
    tgt_copy.start()
    depart(0)
    copy_wait(stage.at[1], stage_sem.at[1])
    hop(1, 0).start()
    depart(1)

    load_gate = pltpu.make_async_copy(w_gate, wgu.at[pl.ds(0, share)], local_sem.at[0])
    load_up = pltpu.make_async_copy(w_up, wgu.at[pl.ds(share, share)], local_sem.at[1])
    load_down = pltpu.make_async_copy(
        w_down.at[:, cols_of(c, half)], wd.at[part], local_sem.at[2]
    )
    load_gate.start()
    load_up.start()
    load_down.start()

    tgt_copy.wait()
    slots = 4 * cap2

    def slot_value(dim, shape):
        r = iota(shape, dim)
        expert = sum((r >= cap2 * k).astype(jnp.int32) for k in range(1, 4))
        rem = r - expert * cap2
        second = (rem >= cap).astype(jnp.int32)
        return (expert * cap + rem - second * cap).astype(F32), second

    def column(line):
        same = iota((tok, tok), 1) == iota((tok, tok), 0)
        lines = jnp.broadcast_to(line, (tok, tok))
        return jnp.sum(jnp.where(same, lines, 0.0), axis=1, keepdims=True)

    value, rel = slot_value(0, (slots, tok))
    lane_value, phase = slot_value(1, (tok, slots))
    for t in range(2):
        here = jnp.where((value == tgt_own[t : t + 1, :]) & (rel == 0), 1.0, 0.0)
        there = jnp.where((value == tgt_far[t : t + 1, :]) & (rel == 1), 1.0, 0.0)
        sel_ref[t] = jnp.concatenate([here, there], axis=1).astype(BF16)
        target = column(tgt_own[t : t + 1, :])
        picks = (lane_value == target) & (phase == t)
        pick_ref[t] = jnp.where(picks, 1.0, 0.0).astype(BF16)
        weight = jnp.where(odd == t, meta_ref[2:3, :], meta_ref[3:4, :])
        weight_ref[t] = jnp.broadcast_to(column(weight), (tok, 128))

    def disp(t, d, j):
        e = turn(d)
        cols = cols_of(j, STEP)
        return remote(
            sendbuf.at[e, :, cols],
            rows_ref.at[t, c * 4 + y, :, cols],
            disp_send.at[d - 1, j],
            disp_recv.at[t, d - 1, j],
            at(e, z, c),
        )

    def disp_left(j):
        for d in (1, 2, 3):
            copy_wait(sendbuf.at[turn(d), :, cols_of(j, STEP)], disp_send.at[d - 1, j])

    def disp_here(t, j):
        cols = cols_of(j, STEP)
        return pltpu.make_async_copy(
            sendbuf.at[y, :, cols], rows_ref.at[t, c * 4 + y, :, cols], disp_local.at[t, j]
        )

    def arrive(t, j):
        passed_on = (t == 1) | (inner == 1)
        copy_wait(xbuf.at[t, 1, :, cols_of(j, STEP)], arr_sem.at[t, j])

        @pl.when(passed_on)
        def _():
            across(t, j).start()

        @pl.when(j == 0)
        def _():
            copy_wait(inv_ref.at[t, 1], inv_sems.at[t, 1])

            @pl.when(passed_on)
            def _():
                inv_across(t).start()

    def dispatch(t, j):
        @pl.when(j == 0)
        def _():
            copy_wait(inv_ref.at[t, 0], inv_sems.at[t, 3])
            for side in range(2):
                inv_col[pl.ds(side * tok, tok), :] = jnp.broadcast_to(
                    column(inv_ref[t, side, 0:1, :]), (tok, 128)
                )

        copy_wait(xbuf.at[t, 0, :, cols_of(j, STEP)], home_sem.at[t, j])

        @pl.when(t == 1)
        def _():
            disp_left(j)

        for i in range(STEP // 512):
            cols = cols_of(i, 512, j * STEP)
            x = xbuf[t, :, :, cols].reshape(2 * tok, 512).astype(F32)
            normed = (x * inv_col[:, 0:1] * gain_ref[:, cols]).astype(BF16)
            picked = jnp.dot(sel_ref[t], normed, preferred_element_type=F32)
            sendbuf[:, :, cols] = picked.astype(BF16).reshape(4, cap2, 512)
        for d in (1, 3, 2):
            disp(t, d, j).start()
        disp_here(t, j).start()

    def cores(t, j):
        block = rows_ref.at[t, pl.ds(c * 4, 4), :, cols_of(j, STEP)]
        return remote(block, block, core_send.at[t], core_recv.at[t, j], at(y, z, 1 - c))

    def share_rows(t, j):
        for d in (1, 3, 2):
            copy_wait(
                rows_ref.at[t, c * 4 + turn(4 - d), :, cols_of(j, STEP)],
                disp_recv.at[t, d - 1, j],
            )
        disp_here(t, j).wait()
        cores(t, j).start()

    def project(t, j):
        cols = cols_of(j, STEP)
        copy_wait(rows_ref.at[t, pl.ds((1 - c) * 4, 4), :, cols], core_recv.at[t, j])

        @pl.when(j == 0)
        def _():
            acc[...] = jnp.zeros_like(acc)

        lhs = rows_ref[t, :, :, cols].reshape(8 * cap2, STEP)
        acc[...] += lax.dot_general(
            lhs, wgu[:, cols], (((1,), (1,)), ((), ())), preferred_element_type=F32
        )

        @pl.when(j == steps - 1)
        def _():
            hidden(t)

    def hid_copy(t, k):
        if k == 0:
            return remote(
                hs.at[t, 0], hid.at[t, part], hid_send.at[t, 0], hid_recv.at[t, 0], at(y, z, 1 - c)
            )
        if k == 1:
            return remote(
                hs.at[t, 1], hid.at[t, part], hid_send.at[t, 1], hid_recv.at[t, 1], (p, far)
            )
        block = hid.at[t, (1 - z) * 2 + c]
        return remote(block, block, hid_send.at[t, 2], hid_recv.at[t, 2], at(y, z, 1 - c))

    def hid_wait(t, k):
        zz, cc = ((z, 1 - c), (1 - z, c), (1 - z, 1 - c))[k]
        copy_wait(hid.at[t, zz * 2 + cc], hid_recv.at[t, k])

    def hidden(t):
        gate, up = acc[:, :share], acc[:, share:]
        h = gate / (1.0 + jnp.exp(-gate)) * up
        mine = [h[b * cap2 : b * cap2 + cap] for b in range(8)]
        others = [h[b * cap2 + cap : (b + 1) * cap2] for b in range(8)]
        hs[t, 1] = jnp.concatenate(others, axis=0).astype(BF16)
        hid_copy(t, 1).start()
        hs[t, 0] = jnp.concatenate(mine, axis=0).astype(BF16)
        hid_copy(t, 0).start()
        hid[t, part] = hs[t, 0]

    def send_down(lo, hi):
        @pl.loop(lo, hi)
        def _(n):
            for k in (1, 2, 0):
                wd_copy(k, n).start()

    load_gate.wait()
    load_up.wait()

    @pl.loop(0, total + LAG + 1)
    def _(k):
        @pl.when(k < total)
        def _():
            arrive(k // steps, k % steps)

        @pl.when(k == total - 1)
        def _():
            send_down(1, EARLY)

        @pl.when((k >= 1) & (k <= total))
        def _():
            dispatch((k - 1) // steps, (k - 1) % steps)

        @pl.when((k >= LAG) & (k < total + LAG))
        def _():
            share_rows((k - LAG) // steps, (k - LAG) % steps)

        @pl.when(k >= LAG + 1)
        def _():
            project((k - LAG - 1) // steps, (k - LAG - 1) % steps)

    send_down(EARLY, out_steps)
    for t in range(2):
        hid_wait(t, 1)
        hid_copy(t, 2).start()
    load_down.wait()
    pl.loop(0, steps)(disp_left)
    for t in range(2):
        hid_wait(t, 0)
        hid_wait(t, 2)

    def back(k, n):
        d, cc = k // 2, k % 2
        to = (c + cc) % 2
        src = sendbuf.at[turn(d), :, cols_of(n, OUT_COLS, to * half)]
        dst = returned.at[y, :, cols_of(n, OUT_COLS, c * half)]
        if k == 0:
            return pltpu.make_async_copy(src, dst, ret_recv.at[c, n])
        return remote(src, dst, ret_send.at[k], ret_recv.at[c, n], at(turn(d), z, to))

    def down(n):
        for k in range(3):
            wd_wait(k, n)
        cols = cols_of(n, OUT_COLS)
        outs = []
        for t in range(2):
            out = jnp.zeros((8 * cap, OUT_COLS), F32)
            for g in range(EGROUP):
                out += jnp.dot(hid[t, g], wd[g, :, cols], preferred_element_type=F32)
            outs.append(out)
        for cc in range(2):
            rows = []
            for b in range(4 * cc, 4 * cc + 4):
                rows += [out[b * cap : (b + 1) * cap] for out in outs]
            sendbuf[:, :, cols_of(n, OUT_COLS, cc * half)] = (
                jnp.concatenate(rows, axis=0).astype(BF16).reshape(4, cap2, OUT_COLS)
            )
        for k in (2, 3, 6, 7, 4, 5, 1, 0):
            back(k, n).start()

    def put(t, ref, side, n):
        cols = cols_of(n, OUT_COLS, side * half)
        return pltpu.make_async_copy(xbuf.at[t, 0, :, cols], ref.at[:, cols], out_sem.at[t])

    def finish(n):
        for side in range(2):
            cols = cols_of(n, OUT_COLS, side * half)
            copy_wait(returned.at[:, :, cols], ret_recv.at[side, n])
            block = returned[:, :, cols].reshape(slots, OUT_COLS)
            for t in range(2):
                taken = jnp.dot(pick_ref[t], block, preferred_element_type=F32)
                home = xbuf[t, 0, :, cols].astype(F32)
                xbuf[t, 0, :, cols] = (home + taken * weight_ref[t][:, 0:1]).astype(BF16)

                @pl.when(odd == t)
                def _():
                    put(t, new_a, side, n).start()

                @pl.when(odd != t)
                def _():
                    put(t, new_b, side, n).start()

    @pl.loop(0, out_steps + BEHIND)
    def _(n):
        @pl.when(n < out_steps)
        def _():
            down(n)

        @pl.when(n >= BEHIND)
        def _():
            finish(n - BEHIND)

    for t in range(2):
        copy_wait(stage.at[t], hi_send.at[t])
        copy_wait(stat.at[t], inv_sems.at[t, 0])

        @pl.when((t == 1) | (inner == 1))
        def _():
            copy_wait(xbuf.at[t, 1], lo_send.at[t])
            copy_wait(inv_ref.at[t, 1], inv_sems.at[t, 2])

        copy_wait(xbuf.at[t, 0], out_sem.at[t])
        copy_wait(rows_ref.at[t, pl.ds(c * 4, 4)], core_send.at[t])
        for k in range(3):
            copy_wait(hs.at[t, 0], hid_send.at[t, k])
    for k in range(3):
        copy_wait(wd.at[part], wd_send.at[k])
    for k in range(1, 8):
        d, cc = k // 2, k % 2
        copy_wait(
            sendbuf.at[turn(d), :, cols_of((c + cc) % 2, half)],
            ret_send.at[k],
        )


def local(
    state_a,
    state_b,
    enter_a,
    enter_b,
    route_a,
    route_b,
    weight_a,
    weight_b,
    norm_gain,
    w_gate,
    w_up,
    w_down,
):
    tok, width = enter_a.shape
    sections = lax.axis_size("pp")
    experts = lax.axis_size("ep") // EGROUP
    cap = tok * 5 // (4 * experts)
    cap2 = 2 * cap
    half = width // 2
    share = w_gate.shape[1]
    steps = width // STEP
    out_steps = half // OUT_COLS
    lines = [v.reshape(1, tok).astype(F32) for v in (route_a, route_b, weight_a, weight_b)]
    meta = jnp.concatenate(lines + [jnp.zeros((4, tok), F32)], axis=0)
    hbm = pl.BlockSpec(memory_space=pl.ANY)
    vmem = pl.BlockSpec(memory_space=pltpu.VMEM)
    dma = pltpu.SemaphoreType.DMA
    new_a, new_b = pl.pallas_call(
        functools.partial(relay_kernel, sections),
        out_shape=(
            jax.ShapeDtypeStruct((tok, width), BF16),
            jax.ShapeDtypeStruct((tok, width), BF16),
        ),
        in_specs=[vmem, vmem] + [hbm] * 7,
        out_specs=(hbm, hbm),
        scratch_shapes=[
            pltpu.VMEM((2, tok, width), BF16),
            pltpu.VMEM((2, 8, tok), F32),
            pltpu.VMEM((tok, 128), F32),
            pltpu.VMEM((2 * tok, 128), F32),
            pltpu.VMEM((2, 2, tok, width), BF16),
            pltpu.VMEM((2, 2, 8, tok), F32),
            pltpu.VMEM((8, tok), F32),
            pltpu.VMEM((8, tok), F32),
            pltpu.VMEM((2, experts * cap2, 2 * tok), BF16),
            pltpu.VMEM((2, tok, experts * cap2), BF16),
            pltpu.VMEM((2, tok, 128), F32),
            pltpu.VMEM((experts, cap2, width), BF16),
            pltpu.VMEM((experts, cap2, width), BF16),
            pltpu.VMEM((2, 8, cap2, width), BF16),
            pltpu.VMEM((2 * share, width), BF16),
            pltpu.VMEM((EGROUP, share, half), BF16),
            pltpu.VMEM((8 * cap2, 2 * share), F32),
            pltpu.VMEM((2, 2, 8 * cap, share), BF16),
            pltpu.VMEM((2, EGROUP, 8 * cap, share), BF16),
            dma((3,)),
            dma((2,)),
            dma((2,)),
            dma((2, 4)),
            dma((2,)),
            dma((2, steps)),
            dma((2, steps)),
            dma((2,)),
            dma((2,)),
            dma((3, steps)),
            dma((2, 3, steps)),
            dma((2, steps)),
            dma((2,)),
            dma((2, steps)),
            dma((2, 3)),
            dma((2, 3)),
            dma((3,)),
            dma((3, out_steps)),
            dma((8,)),
            dma((2, out_steps)),
        ],
        compiler_params=pltpu.CompilerParams(
            collective_id=0, has_side_effects=True, vmem_limit_bytes=60 * 2**20
        ),
        name="relay",
    )(
        meta,
        norm_gain,
        state_a[0],
        state_b[0],
        enter_a,
        enter_b,
        w_gate[0],
        w_up[0],
        w_down[0],
    )
    return (new_a[None], new_b[None])


def solution(mesh):
    return jax.shard_map(
        local,
        mesh=mesh,
        in_specs=(
            P("pp", "ep", None),
            P("pp", "ep", None),
            P("ep", None),
            P("ep", None),
            P("pp", "ep", None),
            P("pp", "ep", None),
            P("pp", "ep", None),
            P("pp", "ep", None),
            P("pp", None),
            P("pp", "ep", None),
            P("pp", "ep", None),
            P("pp", "ep", None),
        ),
        out_specs=(P("pp", "ep", None), P("pp", "ep", None)),
        check_vma=False,
    )
```

time: 705 us -> 197 us (0.28); the launches traced: 691 us -> 193 us
  waiting for transfers between devices: 541 us -> 0 us
  Pallas kernels: 0 us -> 187 us
  matrix products: 55.4 us -> 0 us
  starting transfers between devices: 36.8 us -> 0 us
  other arithmetic: 29.4 us -> 0.68 us
  local copies, waits for them, and re-layouts: 26.9 us -> 5.49 us
    all_to_all x4 -> x0, waiting for transfers between devices: 369 us -> none  [the longest x2 249 us: send_rows(): lax.all_to_all(partial_value, 'ep', split_axis=0, concat_axis=0, tiled=True)]
    pallas_call x0 -> x1, Pallas kernels: none -> 187 us  [local(): pl.pallas_call(functools.partial(relay_kernel, sections), out_shape=(jax....]
    ppermute x2 -> x0, waiting for transfers between devices: 172 us -> none  [passed_along(): return lax.ppermute(block, axis, route)]
    dot_general x6 -> x0, matrix products: 55.4 us -> none  [the longest x2 37.9 us: expert_apply(): jnp.dot(hidden, w_down, preferred_element_type=jnp.float32)]
    all_to_all x4 -> x0, starting transfers between devices: 28.7 us -> none  [the longest x2 14.6 us: send_rows(): lax.all_to_all(outgoing, 'ep', split_axis=0, concat_axis=0, tiled=True)]
    reduce_sum x6 -> x0, other arithmetic: 21.6 us -> none  [the longest x2 16.1 us: send_rows(): return jnp.sum(grouped.astype(jnp.float32), axis=1)]
    gather x2 -> x0, local copies, waits for them, and re-layouts: 14.6 us -> none  [finish(): jnp.take(combined.reshape(-1, width), target, axis=0)]
    broadcast_in_dim x2 -> x1, local copies, waits for them, and re-layouts: 11 us -> 0.01 us  [local(): meta = jnp.concatenate(lines + [jnp.zeros((4, tok), F32)], axis=0)]
  transfers between devices with their start and end apart: 6 -> 0, of which waited for: 6 -> 0; matrix products, arithmetic and copies ran while one was open for 11% -> 0% of each run, Pallas kernels for 0% -> 0%
where the time goes in v2:
time: 197 us; the launch traced here: 193 us
  Pallas kernels  187 us (95%)
  local copies, waits for them, and re-layouts  5.49 us (3%)
    pallas_call x1, Pallas kernels, local(): pl.pallas_call(functools.partial(relay_kernel, sections), out_shape=(jax....  187 us
    unnamed x4, local copies, waits for them, and re-layouts  4.21 us

profile of v2, /device:TPU:7, one launch (start us, length us, event | category | flops | bytes accessed | tf_op | source)
XLA Modules:
  0.0 193.5 jit_solution(12724950741023141437)
XLA Ops:
  0.6 0.7 convert_bitcast_fusion
  1.3 1.3 concatenate.3.meta_ref
  2.6 186.7 %relay.1 = (bf16[128,7168]{1,0:T(8,128)(2,1)}, bf16[128,7168]{1,0:T(8,128)(2,1)}) custom-call(f32[8,128]{1,0:T(8,128)} %concatenate.3.meta_ref, f32[1,7168]{1,0:T(1,128)} %gain_ref.1, bf16[128,7168]{1,0:T(8,128)(2,1)} %bitcast.16, bf16[128,7168]{1,0:T(8,128)(2,1)} %bitcast.17, bf16[128,7168]{1,0:T(8,128)(2,1)} %enter_a.1, bf16[128,7168]{1,0:T(8,128)(2,1)} %enter_b.1, ...), custom_call_target="tpu_custom_call" | custom-call | tf_op jit(solution)/shard_map/relay/pallas_call | solution.py:574
  189.3 0.0 copy-start
  189.3 3.0 %copy.16 = bf16[1,128,7168]{2,1,0:T(8,128)(2,1)} copy(bf16[1,128,7168]{2,1,0:T(8,128)(2,1)} %bitcast.19) | data formatting | bytes 3670016
  192.2 0.0 copy-done
  192.2 1.2 copy.17
  (1 shorter events, 0.0 us)
Async XLA Ops:
  189.3 3.0 %copy-start = (bf16[128,7168]{1,0:T(8,128)(2,1)S(1)}, bf16[128,7168]{1,0:T(8,128)(2,1)}, u32[]{:S(2)}) copy-start(bf16[128,7168]{1,0:T(8,128)(2,1)} %get-tuple-element.5) | copy-start | bytes 5505028

commit v3 on v2

v3 whole, which is shorter than its diff:
```python
import functools

import jax
import jax.numpy as jnp
from jax import lax
from jax.experimental import pallas as pl
from jax.experimental.pallas import tpu as pltpu
from jax.sharding import PartitionSpec as P

EGROUP = 4
MESH = pl.DeviceIdType.MESH
BF16 = jnp.bfloat16
F32 = jnp.float32

STEP = 512
OUT_COLS = 256
LAG = 14
EARLY = 8
BEHIND = 2
AHEAD = 4
NEXT = 3
FILL = (10,)


def iota(shape, dim):
    return lax.broadcasted_iota(jnp.int32, shape, dim)


def copy_wait(ref, sem):
    pltpu.make_async_copy(ref, ref, sem).wait()


def relay_kernel(
    sections,
    route_a_in,
    route_b_in,
    weight_a_in,
    weight_b_in,
    gain_in,
    state_a,
    state_b,
    enter_a,
    enter_b,
    w_gate,
    w_up,
    w_down,
    news,
    route_a,
    route_b,
    weight_a,
    weight_b,
    gain_ref,
    stage,
    stat,
    wide_ref,
    inv_col,
    xbuf,
    inv_ref,
    tgt_own,
    tgt_far,
    sel_ref,
    pick_ref,
    weight_ref,
    sendbuf,
    outbuf,
    returned,
    rows_ref,
    wgu,
    wd,
    acc,
    hs,
    hid,
    local_sem,
    tgt_sems,
    stage_sem,
    inv_sems,
    hi_send,
    arr_sem,
    home_sem,
    lo_send,
    out_sem,
    disp_send,
    disp_recv,
    disp_local,
    core_send,
    core_recv,
    hid_send,
    hid_recv,
    wd_send,
    wd_recv,
    ret_send,
    ret_recv,
):
    tok, width = state_a.shape
    share = w_gate.shape[0]
    half = width // 2
    cap2 = sendbuf.shape[2]
    cap = cap2 // 2
    steps = width // STEP
    total = 2 * steps
    out_steps = half // OUT_COLS

    p = lax.axis_index("pp")
    ep = lax.axis_index("ep")
    y, z, c = ep // 4, (ep // 2) % 2, ep % 2
    odd = p % 2
    inner = (p % (sections - 1) + sections - 2) // (sections - 1)
    edge = inner == 0
    hop_to = (p + inner * (2 * odd - 1), p + 1 - 2 * odd)
    far = y * 4 + (1 - z) * 2 + c
    part = z * 2 + c

    def at(yy, zz, cc):
        return (p, yy * 4 + zz * 2 + cc)

    def turn(d):
        return (y + d) % 4

    def remote(src, dst, send, recv, device):
        return pltpu.make_async_remote_copy(
            src, dst, send, recv, device_id=device, device_id_type=MESH
        )

    def cols_of(i, size, base=0):
        return pl.ds(pl.multiple_of(base + i * size, 128), size)

    barrier = pltpu.get_barrier_semaphore()

    def greet(device):
        pl.semaphore_signal(barrier, inc=1, device_id=device, device_id_type=MESH)

    for d in range(4):
        for cc in range(2):
            if d or cc:
                greet(at(turn(d), z, (c + cc) % 2))
    greet(at(y, 1 - z, c))
    greet(at(y, 1 - z, 1 - c))
    greet((hop_to[1], far))

    @pl.when(inner == 1)
    def _():
        greet((hop_to[0], far))

    def staging(t, ref):
        @pl.loop(0, steps)
        def _(j):
            pltpu.make_async_copy(ref.at[:, cols_of(j, STEP)], stage.at[t, j], stage_sem.at[t]).start()

    @pl.when(edge & (odd == 0))
    def _():
        staging(0, enter_a)

    @pl.when(edge & (odd == 1))
    def _():
        staging(0, enter_b)

    @pl.when((inner == 1) & (odd == 0))
    def _():
        staging(0, state_b)

    @pl.when((inner == 1) & (odd == 1))
    def _():
        staging(0, state_a)

    small = [
        pltpu.make_async_copy(src, dst, local_sem.at[3 + i])
        for i, (src, dst) in enumerate(
            (
                (route_a_in, route_a),
                (route_b_in, route_b),
                (weight_a_in, weight_a),
                (weight_b_in, weight_b),
                (gain_in, gain_ref),
            )
        )
    ]
    for copy in small:
        copy.start()
    pl.semaphore_wait(barrier, 10 + inner)

    def hop(t, j):
        return remote(
            stage.at[t, j], xbuf.at[t, 1, j], hi_send.at[t], arr_sem.at[t, j], (hop_to[t], far)
        )

    def enter_here(j):
        return pltpu.make_async_copy(stage.at[0, j], xbuf.at[0, 0, j], home_sem.at[0, j])

    def across(t, j):
        return remote(
            xbuf.at[t, 1, j], xbuf.at[t, 0, j], lo_send.at[t], home_sem.at[t, j], (p, far)
        )

    def inv_hop(t):
        return remote(
            stat.at[t], inv_ref.at[t, 1], inv_sems.at[t, 0], inv_sems.at[t, 1], (hop_to[t], far)
        )

    def inv_here():
        return pltpu.make_async_copy(stat.at[0], inv_ref.at[0, 0], inv_sems.at[0, 3])

    def inv_across(t):
        return remote(
            inv_ref.at[t, 1], inv_ref.at[t, 0], inv_sems.at[t, 2], inv_sems.at[t, 3], (p, far)
        )

    def depart(t):
        wide_ref[...] = jnp.zeros_like(wide_ref)

        @pl.loop(0, steps)
        def _(j):
            for i in range(STEP // 128):
                block = stage[t, j, :, i * 128 : (i + 1) * 128].astype(F32)
                wide_ref[...] += block * block

        mean = jnp.sum(wide_ref[...], axis=1, keepdims=True) * (1.0 / width)
        same = iota((tok, tok), 1) == iota((tok, tok), 0)
        line = jnp.sum(jnp.where(same, lax.rsqrt(mean + 1e-06), 0.0), axis=0, keepdims=True)
        stat[t] = jnp.broadcast_to(line, (8, tok))
        inv_hop(t).start()

        @pl.loop(2 - t, steps)
        def _(j):
            hop(t, j).start()

        if t == 0:

            @pl.when(edge)
            def _():
                inv_here().start()

                @pl.loop(0, steps)
                def _(j):
                    enter_here(j).start()

    def wd_other(k):
        return (z, 1 - c) if k == 0 else (1 - z, c if k == 1 else 1 - c)

    pair = 2 * OUT_COLS
    pairs = out_steps // 2

    def wd_copy(k, m):
        zz, cc = wd_other(k)
        return remote(
            w_down.at[:, cols_of(m, pair, cc * half)],
            wd.at[part, m],
            wd_send.at[k],
            wd_recv.at[k, m],
            at(y, zz, cc),
        )

    def wd_copy_last(k, i):
        zz, cc = wd_other(k)
        return remote(
            w_down.at[:, cols_of(out_steps - 2 + i, OUT_COLS, cc * half)],
            wd.at[part, pairs - 1, :, i * OUT_COLS : (i + 1) * OUT_COLS],
            wd_send.at[k],
            wd_recv.at[k, pairs - 1 + i],
            at(y, zz, cc),
        )

    def wd_wait(k, n):
        zz, cc = wd_other(k)

        @pl.when((n % 2 == 0) & (n < out_steps - 2))
        def _():
            copy_wait(wd.at[zz * 2 + cc, n // 2], wd_recv.at[k, n // 2])

        for i in range(2):

            @pl.when(n == out_steps - 2 + i)
            def _():
                block = wd.at[zz * 2 + cc, pairs - 1, :, i * OUT_COLS : (i + 1) * OUT_COLS]
                copy_wait(block, wd_recv.at[k, pairs - 1 + i])

    for k in (1, 0):
        wd_copy(k, 0).start()
    copy_wait(stage.at[0], stage_sem.at[0])
    hop(0, 0).start()
    hop(0, 1).start()
    @pl.when(odd == 0)
    def _():
        staging(1, state_a)

    @pl.when(odd == 1)
    def _():
        staging(1, state_b)

    for copy in small:
        copy.wait()
    tri = (iota((tok, tok), 0) < iota((tok, tok), 1)).astype(BF16)
    slot_rows = []
    for t in range(2):
        route = jnp.where(odd == t, route_a[...], route_b[...]).astype(F32)
        onehot = (iota((16, tok), 0).astype(F32) == route).astype(F32)
        earlier = jnp.dot(onehot.astype(BF16), tri, preferred_element_type=F32)
        rank = jnp.sum(onehot * earlier, axis=0, keepdims=True)
        slot_rows.append(route * cap + rank)
    tgt_own[...] = jnp.concatenate(slot_rows + [jnp.zeros((6, tok), F32)], axis=0)
    tgt_copy = remote(tgt_own, tgt_far, tgt_sems.at[0], tgt_sems.at[1], (p, far))
    tgt_copy.start()
    depart(0)
    copy_wait(stage.at[1], stage_sem.at[1])
    hop(1, 0).start()
    depart(1)

    load_gate = pltpu.make_async_copy(w_gate, wgu.at[pl.ds(0, share)], local_sem.at[0])
    load_up = pltpu.make_async_copy(w_up, wgu.at[pl.ds(share, share)], local_sem.at[1])
    load_gate.start()
    load_up.start()

    @pl.loop(0, out_steps // 2)
    def _(m):
        pltpu.make_async_copy(
            w_down.at[:, cols_of(m, 2 * OUT_COLS, c * half)], wd.at[part, m], local_sem.at[2]
        ).start()

    tgt_copy.wait()
    slots = 4 * cap
    r = iota((2 * slots, tok), 0)
    expert = sum((r >= cap2 * k).astype(jnp.int32) for k in range(1, 4))
    rem = r - expert * cap2
    rel = (rem >= cap).astype(jnp.int32)
    value = (expert * cap + rem - rel * cap).astype(F32)

    def column(line):
        same = iota((tok, tok), 1) == iota((tok, tok), 0)
        lines = jnp.broadcast_to(line, (tok, tok))
        return jnp.sum(jnp.where(same, lines, 0.0), axis=1, keepdims=True)

    for t in range(2):
        here = jnp.where((value == tgt_own[t : t + 1, :]) & (rel == 0), 1.0, 0.0)
        there = jnp.where((value == tgt_far[t : t + 1, :]) & (rel == 1), 1.0, 0.0)
        sel_ref[t] = jnp.concatenate([here, there], axis=1).astype(BF16)
        target = column(tgt_own[t : t + 1, :])
        picks = iota((tok, slots), 1).astype(F32) == target
        pick_ref[t] = jnp.where(picks, 1.0, 0.0).astype(BF16)
        weight = jnp.where(odd == t, weight_a[...], weight_b[...])
        weight_ref[t] = jnp.broadcast_to(column(weight), (tok, 128))

    def disp(t, d, j):
        e = turn(d)
        return remote(
            sendbuf.at[j, e],
            rows_ref.at[t, j, c * 4 + y],
            disp_send.at[d - 1, j],
            disp_recv.at[t, d - 1, j],
            at(e, z, c),
        )

    def disp_left(j):
        for d in (1, 2, 3):
            copy_wait(sendbuf.at[j, turn(d)], disp_send.at[d - 1, j])

    def disp_here(t, j):
        return pltpu.make_async_copy(
            sendbuf.at[j, y], rows_ref.at[t, j, c * 4 + y], disp_local.at[t, j]
        )

    def arrive(t, j):
        passed_on = (t == 1) | (inner == 1)
        copy_wait(xbuf.at[t, 1, j], arr_sem.at[t, j])

        @pl.when(passed_on)
        def _():
            across(t, j).start()

        @pl.when(j == 0)
        def _():
            copy_wait(inv_ref.at[t, 1], inv_sems.at[t, 1])

            @pl.when(passed_on)
            def _():
                inv_across(t).start()

    def dispatch(t, j):
        @pl.when(j == 0)
        def _():
            copy_wait(inv_ref.at[t, 0], inv_sems.at[t, 3])
            for side in range(2):
                inv_col[pl.ds(side * tok, tok), :] = jnp.broadcast_to(
                    column(inv_ref[t, side, 0:1, :]), (tok, 128)
                )

        copy_wait(xbuf.at[t, 0, j], home_sem.at[t, j])

        @pl.when(t == 1)
        def _():
            disp_left(j)

        x = xbuf[t, :, j].reshape(2 * tok, STEP).astype(F32)
        normed = (x * inv_col[:, 0:1] * gain_ref[:, cols_of(j, STEP)]).astype(BF16)
        picked = jnp.dot(sel_ref[t], normed, preferred_element_type=F32)
        sendbuf[j] = picked.astype(BF16).reshape(4, cap2, STEP)
        for d in (1, 3, 2):
            disp(t, d, j).start()
        disp_here(t, j).start()

    def cores(t, j):
        block = rows_ref.at[t, j, pl.ds(c * 4, 4)]
        return remote(block, block, core_send.at[t], core_recv.at[t, j], at(y, z, 1 - c))

    def share_rows(t, j):
        for d in (1, 3, 2):
            copy_wait(rows_ref.at[t, j, c * 4 + turn(4 - d)], disp_recv.at[t, d - 1, j])
        disp_here(t, j).wait()
        cores(t, j).start()

    def project(t, j):
        cols = cols_of(j, STEP)
        copy_wait(rows_ref.at[t, j, pl.ds((1 - c) * 4, 4)], core_recv.at[t, j])

        @pl.when(j == 0)
        def _():
            acc[...] = jnp.zeros_like(acc)

        lhs = rows_ref[t, j].reshape(8 * cap2, STEP)
        acc[...] += lax.dot_general(
            lhs, wgu[:, cols], (((1,), (1,)), ((), ())), preferred_element_type=F32
        )

        @pl.when(j == steps - 1)
        def _():
            hidden(t)

    def hid_copy(t, k):
        if k == 0:
            return remote(
                hs.at[t, 0], hid.at[t, part], hid_send.at[t, 0], hid_recv.at[t, 0], at(y, z, 1 - c)
            )
        if k == 1:
            return remote(
                hs.at[t, 1], hid.at[t, part], hid_send.at[t, 1], hid_recv.at[t, 1], (p, far)
            )
        block = hid.at[t, (1 - z) * 2 + c]
        return remote(block, block, hid_send.at[t, 2], hid_recv.at[t, 2], at(y, z, 1 - c))

    def hid_wait(t, k):
        zz, cc = ((z, 1 - c), (1 - z, c), (1 - z, 1 - c))[k]
        copy_wait(hid.at[t, zz * 2 + cc], hid_recv.at[t, k])

    def hidden(t):
        gate, up = acc[:, :share], acc[:, share:]
        h = gate / (1.0 + jnp.exp(-gate)) * up
        mine = [h[b * cap2 : b * cap2 + cap] for b in range(8)]
        others = [h[b * cap2 + cap : (b + 1) * cap2] for b in range(8)]
        hs[t, 1] = jnp.concatenate(others, axis=0).astype(BF16)
        hid_copy(t, 1).start()
        hs[t, 0] = jnp.concatenate(mine, axis=0).astype(BF16)
        hid_copy(t, 0).start()
        hid[t, part] = hs[t, 0]

    def send_down(lo, hi):
        @pl.loop(lo, hi)
        def _(m):
            for k in (1, 2, 0):
                wd_copy(k, m).start()

    def send_down_rest():
        send_down(EARLY // 2, pairs - 1)
        for i in range(2):
            for k in (1, 2, 0):
                wd_copy_last(k, i).start()

    def back(t, k, n):
        d, cc = k // 2, k % 2
        to = (c + cc) % 2
        src = outbuf.at[t, n, to * 4 + turn(d)]
        dst = returned.at[t, n, c, y]
        if k == 0:
            return pltpu.make_async_copy(src, dst, ret_recv.at[t, c, n])
        return remote(src, dst, ret_send.at[t, k], ret_recv.at[t, c, n], at(turn(d), z, to))

    def down_wait(n):
        for k in range(3):
            wd_wait(k, n)

    def down(t, n):
        cols = cols_of(n % 2, OUT_COLS)
        out = jnp.zeros((8 * cap, OUT_COLS), F32)
        for g in range(EGROUP):
            out += jnp.dot(hid[t, g], wd[g, n // 2, :, cols], preferred_element_type=F32)
        outbuf[t, n] = out.reshape(8, cap, OUT_COLS).astype(BF16)
        for k in (2, 3, 6, 7, 4, 5, 1, 0):
            back(t, k, n).start()

    def pass_hidden(t):
        hid_wait(t, 1)
        hid_copy(t, 2).start()

    def have_hidden(t):
        hid_wait(t, 0)
        hid_wait(t, 2)

    def place(side, n):
        at_step = n // (STEP // OUT_COLS)
        return side * (half // STEP) + at_step, cols_of(n % (STEP // OUT_COLS), OUT_COLS)

    def put(t, side, n):
        j, cols = place(side, n)
        return pltpu.make_async_copy(
            xbuf.at[t, 0, j, :, cols],
            news.at[(t + odd) % 2, :, cols_of(n, OUT_COLS, side * half)],
            out_sem.at[t],
        )

    def finish(n):
        for side in range(2):
            j, cols = place(side, n)
            for t in range(2):
                copy_wait(returned.at[t, n, side], ret_recv.at[t, side, n])
                block = returned[t, n, side].astype(F32).reshape(slots, OUT_COLS)
                taken = jnp.dot(pick_ref[t], block.astype(BF16), preferred_element_type=F32)
                home = xbuf[t, 0, j, :, cols].astype(F32)
                xbuf[t, 0, j, :, cols] = (home + taken * weight_ref[t][:, 0:1]).astype(BF16)
                put(t, side, n).start()

    load_gate.wait()
    load_up.wait()
    copy_wait(wd.at[part], local_sem.at[2])

    @pl.loop(0, total + LAG + 1)
    def _(k):
        @pl.when(k < total)
        def _():
            arrive(k // steps, k % steps)

        @pl.when((k >= NEXT) & (k < total + NEXT))
        def _():
            dispatch((k - NEXT) // steps, (k - NEXT) % steps)

        @pl.when((k >= LAG) & (k < total + LAG))
        def _():
            share_rows((k - LAG) // steps, (k - LAG) % steps)

        @pl.when(k >= LAG + 1)
        def _():
            project((k - LAG - 1) // steps, (k - LAG - 1) % steps)

        @pl.when(k == 2)
        def _():
            wd_copy(2, 0).start()

        for n, when in enumerate(FILL, 1):

            @pl.when(k == when)
            def _():
                send_down(n, n + 1)

        @pl.when(k == steps + LAG)
        def _():
            send_down(1 + len(FILL), EARLY // 2)

        @pl.when(k == total + LAG - AHEAD - 2)
        def _():
            pass_hidden(0)

        @pl.when(k == total + LAG - AHEAD)
        def _():
            have_hidden(0)

        @pl.when((k >= total + LAG - AHEAD) & (k < total + LAG))
        def _():
            down_wait(k - (total + LAG - AHEAD))
            down(0, k - (total + LAG - AHEAD))

    send_down_rest()

    @pl.loop(AHEAD, EARLY - 1)
    def _(n):
        down_wait(n)
        down(0, n)

    pass_hidden(1)
    down_wait(EARLY - 1)
    down(0, EARLY - 1)
    have_hidden(1)

    @pl.loop(0, out_steps + BEHIND)
    def _(n):
        @pl.when(n < out_steps)
        def _():
            down(1, n)

        @pl.when((n >= EARLY - 1) & (n < out_steps - 1))
        def _():
            down_wait(n + 1)
            down(0, n + 1)

        @pl.when(n >= BEHIND)
        def _():
            finish(n - BEHIND)

    for t in range(2):
        copy_wait(stage.at[t], hi_send.at[t])
        copy_wait(stat.at[t], inv_sems.at[t, 0])

        @pl.when((t == 1) | (inner == 1))
        def _():
            copy_wait(xbuf.at[t, 1], lo_send.at[t])
            copy_wait(inv_ref.at[t, 1], inv_sems.at[t, 2])

        copy_wait(xbuf.at[t, 0], out_sem.at[t])
        copy_wait(rows_ref.at[t, :, pl.ds(c * 4, 4)], core_send.at[t])
        for k in range(3):
            copy_wait(hs.at[t, 0], hid_send.at[t, k])
    for k in range(3):
        copy_wait(wd.at[part], wd_send.at[k])
    pl.loop(0, steps)(disp_left)
    for t in range(2):
        for k in range(1, 8):
            d, cc = k // 2, k % 2
            copy_wait(outbuf.at[t, :, ((c + cc) % 2) * 4 + turn(d)], ret_send.at[t, k])


def local(
    state_a,
    state_b,
    enter_a,
    enter_b,
    route_a,
    route_b,
    weight_a,
    weight_b,
    norm_gain,
    w_gate,
    w_up,
    w_down,
):
    tok, width = enter_a.shape
    sections = lax.axis_size("pp")
    experts = lax.axis_size("ep") // EGROUP
    cap = tok * 5 // (4 * experts)
    cap2 = 2 * cap
    half = width // 2
    share = w_gate.shape[1]
    steps = width // STEP
    out_steps = half // OUT_COLS
    lines = [v.reshape(1, tok) for v in (route_a, route_b, weight_a, weight_b)]
    hbm = pl.BlockSpec(memory_space=pl.ANY)
    dma = pltpu.SemaphoreType.DMA
    news = pl.pallas_call(
        functools.partial(relay_kernel, sections),
        out_shape=jax.ShapeDtypeStruct((2, tok, width), BF16),
        in_specs=[hbm] * 12,
        out_specs=hbm,
        scratch_shapes=[
            pltpu.VMEM((1, tok), jnp.int32),
            pltpu.VMEM((1, tok), jnp.int32),
            pltpu.VMEM((1, tok), F32),
            pltpu.VMEM((1, tok), F32),
            pltpu.VMEM((1, width), F32),
            pltpu.VMEM((2, steps, tok, STEP), BF16),
            pltpu.VMEM((2, 8, tok), F32),
            pltpu.VMEM((tok, 128), F32),
            pltpu.VMEM((2 * tok, 128), F32),
            pltpu.VMEM((2, 2, steps, tok, STEP), BF16),
            pltpu.VMEM((2, 2, 8, tok), F32),
            pltpu.VMEM((8, tok), F32),
            pltpu.VMEM((8, tok), F32),
            pltpu.VMEM((2, experts * cap2, 2 * tok), BF16),
            pltpu.VMEM((2, tok, experts * cap), BF16),
            pltpu.VMEM((2, tok, 128), F32),
            pltpu.VMEM((steps, experts, cap2, STEP), BF16),
            pltpu.VMEM((2, out_steps, 8, cap, OUT_COLS), BF16),
            pltpu.VMEM((2, out_steps, 2, experts, cap, OUT_COLS), BF16),
            pltpu.VMEM((2, steps, 8, cap2, STEP), BF16),
            pltpu.VMEM((2 * share, width), BF16),
            pltpu.VMEM((EGROUP, out_steps // 2, share, 2 * OUT_COLS), BF16),
            pltpu.VMEM((8 * cap2, 2 * share), F32),
            pltpu.VMEM((2, 2, 8 * cap, share), BF16),
            pltpu.VMEM((2, EGROUP, 8 * cap, share), BF16),
            dma((8,)),
            dma((2,)),
            dma((2,)),
            dma((2, 4)),
            dma((2,)),
            dma((2, steps)),
            dma((2, steps)),
            dma((2,)),
            dma((2,)),
            dma((3, steps)),
            dma((2, 3, steps)),
            dma((2, steps)),
            dma((2,)),
            dma((2, steps)),
            dma((2, 3)),
            dma((2, 3)),
            dma((3,)),
            dma((3, out_steps // 2 + 1)),
            dma((2, 8)),
            dma((2, 2, out_steps)),
        ],
        compiler_params=pltpu.CompilerParams(
            collective_id=0, has_side_effects=True, vmem_limit_bytes=62 * 2**20
        ),
        name="relay",
    )(
        *lines,
        norm_gain,
        state_a[0],
        state_b[0],
        enter_a,
        enter_b,
        w_gate[0],
        w_up[0],
        w_down[0],
    )
    return (news[0:1], news[1:2])


def solution(mesh):
    return jax.shard_map(
        local,
        mesh=mesh,
        in_specs=(
            P("pp", "ep", None),
            P("pp", "ep", None),
            P("ep", None),
            P("ep", None),
            P("pp", "ep", None),
            P("pp", "ep", None),
            P("pp", "ep", None),
            P("pp", "ep", None),
            P("pp", None),
            P("pp", "ep", None),
            P("pp", "ep", None),
            P("pp", "ep", None),
        ),
        out_specs=(P("pp", "ep", None), P("pp", "ep", None)),
        check_vma=False,
    )
```

time: 197 us -> 191 us (0.970); the launches traced: 193 us -> 191 us
    unnamed x4 -> x0, local copies, waits for them, and re-layouts: 4.21 us -> none
    slice x0 -> x1, local copies, waits for them, and re-layouts: none -> 4.12 us  [local(): return (news[0:1], news[1:2])]
where the time goes in v3:
time: 191 us
  Pallas kernels  186 us (97%)
  local copies, waits for them, and re-layouts  4.12 us (2%)
    pallas_call x1, Pallas kernels, local(): pl.pallas_call(functools.partial(relay_kernel, sections), out_shape=jax.S...  186 us
    slice x1, local copies, waits for them, and re-layouts, local(): return (news[0:1], news[1:2])  4.12 us

profile of v3, /device:TPU:7, one launch (start us, length us, event | category | flops | bytes accessed | tf_op | source)
XLA Modules:
  0.0 190.7 jit_solution(3224090793579278416)
XLA Ops:
  0.6 185.9 %relay.1 = bf16[2,128,7168]{2,1,0:T(8,128)(2,1)} custom-call(s32[1,128]{1,0:T(1,128)} %bitcast.14, s32[1,128]{1,0:T(1,128)} %bitcast.15, f32[1,128]{1,0:T(1,128)} %bitcast.16, f32[1,128]{1,0:T(1,128)} %bitcast.17, f32[1,7168]{1,0:T(1,128)} %gain_in.1, bf16[128,7168]{1,0:T(8,128)(2,1)} %bitcast.12, bf16[128,7168]{1,0:T(8,128)(2,1)} %bitcast.13, ...), custom_call_target="tpu_custom_call" | custom-call | tf_op jit(solution)/shard_map/relay/pallas_call | solution.py:642
  186.5 4.1 %fusion = (bf16[1,128,7168]{2,1,0:T(8,128)(2,1)}, bf16[1,128,7168]{2,1,0:T(8,128)(2,1)}) fusion(bf16[2,128,7168]{2,1,0:T(8,128)(2,1)} %relay.1), kind=kLoop, calls=%fused_computation | loop fusion | bytes 7340032 | tf_op jit(solution)/shard_map/slice | solution.py:709

commit v4 on v3

--- a/solution.py
+++ b/solution.py
@@ -16,7 +16,6 @@
 OUT_COLS = 256
 LAG = 14
 EARLY = 8
-BEHIND = 2
 AHEAD = 4
 NEXT = 3
 FILL = (10,)
@@ -481,7 +480,7 @@
         for g in range(EGROUP):
             out += jnp.dot(hid[t, g], wd[g, n // 2, :, cols], preferred_element_type=F32)
         outbuf[t, n] = out.reshape(8, cap, OUT_COLS).astype(BF16)
-        for k in (2, 3, 6, 7, 4, 5, 1, 0):
+        for k in (4, 5, 2, 3, 6, 7, 1, 0):
             back(t, k, n).start()
 
     def pass_hidden(t):
@@ -576,20 +575,19 @@
     down(0, EARLY - 1)
     have_hidden(1)
 
-    @pl.loop(0, out_steps + BEHIND)
+    @pl.loop(0, EARLY)
     def _(n):
-        @pl.when(n < out_steps)
-        def _():
-            down(1, n)
-
-        @pl.when((n >= EARLY - 1) & (n < out_steps - 1))
-        def _():
-            down_wait(n + 1)
-            down(0, n + 1)
-
-        @pl.when(n >= BEHIND)
-        def _():
-            finish(n - BEHIND)
+        down(1, n)
+
+    @pl.loop(EARLY, out_steps)
+    def _(n):
+        finish(2 * (n - EARLY))
+        finish(2 * (n - EARLY) + 1)
+        down_wait(n)
+        for t in range(2):
+            down(t, n)
+
+    pl.loop(2 * (out_steps - EARLY), out_steps)(finish)
 
     for t in range(2):
         copy_wait(stage.at[t], hi_send.at[t])

time: 191 us -> 190 us (level)
  no operation moved by 1% of the time
where the time goes in v4:
time: 190 us
  Pallas kernels  186 us (98%)
  local copies, waits for them, and re-layouts  4.12 us (2%)
    pallas_call x1, Pallas kernels, local(): pl.pallas_call(functools.partial(relay_kernel, sections), out_shape=jax.S...  186 us
    slice x1, local copies, waits for them, and re-layouts, local(): return (news[0:1], news[1:2])  4.12 us

profile of v4, /device:TPU:7, one launch (start us, length us, event | category | flops | bytes accessed | tf_op | source)
XLA Modules:
  0.0 190.3 jit_solution(13049213444862534921)
XLA Ops:
  0.6 185.6 %relay.1 = bf16[2,128,7168]{2,1,0:T(8,128)(2,1)} custom-call(s32[1,128]{1,0:T(1,128)} %bitcast.14, s32[1,128]{1,0:T(1,128)} %bitcast.15, f32[1,128]{1,0:T(1,128)} %bitcast.16, f32[1,128]{1,0:T(1,128)} %bitcast.17, f32[1,7168]{1,0:T(1,128)} %gain_in.1, bf16[128,7168]{1,0:T(8,128)(2,1)} %bitcast.12, bf16[128,7168]{1,0:T(8,128)(2,1)} %bitcast.13, ...), custom_call_target="tpu_custom_call" | custom-call | tf_op jit(solution)/shard_map/relay/pallas_call | solution.py:640
  186.2 4.1 %fusion = (bf16[1,128,7168]{2,1,0:T(8,128)(2,1)}, bf16[1,128,7168]{2,1,0:T(8,128)(2,1)}) fusion(bf16[2,128,7168]{2,1,0:T(8,128)(2,1)} %relay.1), kind=kLoop, calls=%fused_computation | loop fusion | bytes 7340032 | tf_op jit(solution)/shard_map/slice | solution.py:707
